TPU v7x, 32 devices: a whole 2x2x4 slice. The times are simulated.
32 devices in a mesh: node: 8 (over z, x), local: 4 (over y, core).
Axes of the slice: x: 2, y: 2, z: 4, core: 2. Of those that a mesh axis runs over, the one named last changes fastest.
Arguments:
- layer_input: bfloat16 [1024, 3584], P('node', 'local'), may hold values from -6 to 6
- output_grad: bfloat16 [1024, 3584], P('node', 'local'), may hold values from -6 to 6
- gate_weight: bfloat16 [8, 3584, 1024], P('node', None, 'local'), may hold values from -0.09375 to 0.09375
- up_weight: bfloat16 [8, 3584, 1024], P('node', None, 'local'), may hold values from -0.09375 to 0.09375
- down_weight: bfloat16 [8, 1024, 3584], P('node', 'local'), may hold values from -0.1875 to 0.1875
- route_offset: int32 [1024, 2], P('node'), may hold values from 0 to 3, all different within a row; in each aligned block of 128 rows (0 to 127, 128 to 255, ...) at most 80 rows name the same one
- gate_fixed: int32 [1024, 2], P('node'), may hold values from 4096 to 65535
Outputs:
- input_grad: bfloat16 [1024, 3584], P('node', 'local')
- gate_grad: float32 [1024, 2], P('node')
Inputs may be any that keep to these rules, and one draw needn't show every extreme that they name: `route_offset`: each token names 2 different offsets. Among the 128 tokens of one node no offset is named more than 80 times, and in some node one offset is named exactly 80 times.
All inputs are finite; a program needn't handle non-finite values.
Results may differ from a plain program's by a relative error of at most 0.0049.
Values may be sent and summed in bfloat16 or wider, within the bound.
A program may use at most 64 MiB of HBM per device.

v0:
```python
import jax
import jax.numpy as jnp
from jax import lax
from jax.sharding import PartitionSpec as P

GROUP = 4
CAPACITY = 80


def from_behind(value, axis, steps):
    count = lax.axis_size(axis)
    pairs = [(source, (source + steps) % count) for source in range(count)]
    return lax.ppermute(value, axis, pairs)


def packer(chosen, capacity):
    ranks = jnp.cumsum(chosen.astype(jnp.int32)) - 1
    slots = jnp.arange(capacity, dtype=jnp.int32)
    return ((ranks[None, :] == slots[:, None]) & chosen[None, :]).astype(jnp.bfloat16)


def hidden_grads(rows_in, rows_grad, gate_cols, up_cols, down_rows):
    gate_pre = jnp.dot(rows_in, gate_cols, preferred_element_type=jnp.float32)
    up_pre = jnp.dot(rows_in, up_cols, preferred_element_type=jnp.float32)
    hidden_grad = lax.dot_general(
        rows_grad, down_rows, (((1,), (1,)), ((), ())), preferred_element_type=jnp.float32
    )
    sigmoid = jax.nn.sigmoid(gate_pre)
    swish = gate_pre * sigmoid
    gate_part = jnp.sum(swish * up_pre * hidden_grad, axis=1)
    up_grad = (hidden_grad * swish).astype(jnp.bfloat16)
    pre_grad = (hidden_grad * up_pre * sigmoid * (1.0 + gate_pre * (1.0 - sigmoid))).astype(
        jnp.bfloat16
    )
    return (gate_part, up_grad, pre_grad)


def carry_out(first, second):
    got_first = [first[0]]
    got_second = [second[0]]
    for offset in range(1, GROUP):
        moved_first, moved_second = from_behind((first[offset], second[offset]), "node", offset)
        got_first.append(moved_first)
        got_second.append(moved_second)
    return (jnp.stack(got_first), jnp.stack(got_second))


def carry_home(first, second):
    got_first = [first[0]]
    got_second = [second[0]]
    for offset in range(1, GROUP):
        moved_first, moved_second = from_behind((first[offset], second[offset]), "node", -offset)
        got_first.append(moved_first)
        got_second.append(moved_second)
    return (jnp.stack(got_first), jnp.stack(got_second))


def body(layer_input, output_grad, gate_weight, up_weight, down_weight, route_offset, gate_fixed):
    local_count = lax.axis_size("local")
    gate_cols = gate_weight[0]
    up_cols = up_weight[0]
    down_rows = down_weight[0]
    gates = gate_fixed.astype(jnp.float32) / 65536.0
    slot_list = []
    weights = []
    hit_list = []
    packed_in = []
    packed_grad = []
    for offset in range(GROUP):
        hits = route_offset == offset
        chosen = jnp.any(hits, axis=1)
        table = packer(chosen, CAPACITY)
        ranks = jnp.cumsum(chosen.astype(jnp.int32)) - 1
        slot_list.append(jnp.clip(ranks, 0, CAPACITY - 1))
        hit_list.append(hits)
        weights.append(jnp.sum(jnp.where(hits, gates, jnp.zeros_like(gates)), axis=1))
        packed_in.append(
            jnp.dot(table, layer_input, preferred_element_type=jnp.float32).astype(jnp.bfloat16)
        )
        packed_grad.append(
            jnp.dot(table, output_grad, preferred_element_type=jnp.float32).astype(jnp.bfloat16)
        )
    send_in = jnp.stack(packed_in)
    send_grad = jnp.stack(packed_grad)
    got_in, got_grad = carry_out(send_in, send_grad)
    got_in, got_grad = (
        lax.all_gather(got_in, "local", axis=2, tiled=True),
        lax.all_gather(got_grad, "local", axis=2, tiled=True),
    )
    width = got_in.shape[2]
    routed = GROUP * CAPACITY
    flat_in = got_in.reshape(routed, width)
    flat_grad = got_grad.reshape(routed, width)
    gate_part, up_grad, pre_grad = hidden_grads(flat_in, flat_grad, gate_cols, up_cols, down_rows)
    joined_grad = jnp.concatenate((pre_grad, up_grad), axis=1)
    joined_cols = jnp.concatenate((gate_cols, up_cols), axis=1)
    back = lax.dot_general(
        joined_grad, joined_cols, (((1,), (1,)), ((), ())), preferred_element_type=jnp.float32
    )
    gate_wide = jnp.broadcast_to(gate_part[:, None], (routed, local_count))
    summed, gate_sum = (
        lax.psum_scatter(
            back.reshape(GROUP, CAPACITY, width), "local", scatter_dimension=2, tiled=True
        ),
        lax.psum_scatter(
            gate_wide.reshape(GROUP, CAPACITY, local_count),
            "local",
            scatter_dimension=2,
            tiled=True,
        ),
    )
    home_back, home_gate = carry_home(summed, gate_sum)
    input_acc = jnp.zeros(layer_input.shape, jnp.float32)
    gate_acc = jnp.zeros(gate_fixed.shape, jnp.float32)
    for offset in range(GROUP):
        rows_back = jnp.take(home_back[offset], slot_list[offset], axis=0)
        gate_back = jnp.take(home_gate[offset], slot_list[offset], axis=0)
        input_acc = input_acc + weights[offset][:, None] * rows_back
        gate_acc = gate_acc + jnp.where(hit_list[offset], gate_back, jnp.zeros_like(gate_acc))
    return (input_acc.astype(jnp.bfloat16), gate_acc)


def solution(mesh):
    in_specs = (
        P("node", "local"),
        P("node", "local"),
        P("node", None, "local"),
        P("node", None, "local"),
        P("node", "local", None),
        P("node", None),
        P("node", None),
    )
    out_specs = (P("node", "local"), P("node", None))
    return jax.shard_map(body, mesh=mesh, in_specs=in_specs, out_specs=out_specs, check_vma=False)
```

profile of v0, /device:TPU:26, one launch (start us, length us, event | category | flops | bytes accessed | tf_op | source)
XLA Modules:
  0.0 173.2 jit_solution(11934670922993045439)
XLA Ops:
  11.5 2.5 %collective-permute-start.4 = (bf16[80,896]{1,0:T(8,128)(2,1)S(1)}, bf16[80,896]{1,0:T(8,128)(2,1)S(1)}, u32[]{:S(2)}, u32[]{:S(2)}) collective-permute-start(bf16[80,896]{1,0:T(8,128)(2,1)S(1)} %convolution_convert_fusion.1), channel_id=1, source_target_pairs={{0,8},{4,12},{8,16},{12,20},{16,24},{20,28},{24,0},{28,4},{1,9},{5... | collective-permute-start | bytes 430088 | tf_op jit(solution)/shard_map/ppermute | solution.py:13
  15.6 1.5 collective-permute-start.3
  17.7 2.7 %collective-permute-done.4 = bf16[80,896]{1,0:T(8,128)(2,1)S(1)} collective-permute-done((bf16[80,896]{1,0:T(8,128)(2,1)S(1)}, bf16[80,896]{1,0:T(8,128)(2,1)S(1)}, u32[]{:S(2)}, u32[]{:S(2)}) %collective-permute-start.4) | collective-permute-done | bytes 143392 | tf_op jit(solution)/shard_map/ppermute | solution.py:13
  21.9 2.9 %collective-permute-start.2 = (bf16[80,896]{1,0:T(8,128)(2,1)S(1)}, bf16[80,896]{1,0:T(8,128)(2,1)S(1)}, u32[]{:S(2)}, u32[]{:S(2)}) collective-permute-start(bf16[80,896]{1,0:T(8,128)(2,1)S(1)} %convolution_convert_fusion.4), channel_id=1, source_target_pairs={{0,12},{4,16},{8,20},{12,24},{16,28},{20,0},{24,4},{28,8},{1,13},{... | collective-permute-start | bytes 430088 | tf_op jit(solution)/shard_map/ppermute | solution.py:13
  25.0 5.5 %collective-permute-start.1 = (bf16[80,896]{1,0:T(8,128)(2,1)S(1)}, bf16[80,896]{1,0:T(8,128)(2,1)S(1)}, u32[]{:S(2)}, u32[]{:S(2)}) collective-permute-start(bf16[80,896]{1,0:T(8,128)(2,1)S(1)} %convolution_convert_fusion.5), channel_id=1, source_target_pairs={{0,8},{4,12},{8,16},{12,20},{16,24},{20,28},{24,0},{28,4},{1,9},{5... | collective-permute-start | bytes 430088 | tf_op jit(solution)/shard_map/ppermute | solution.py:13
  30.9 1.5 collective-permute-done.2
  32.5 2.2 %collective-permute-done.1 = bf16[80,896]{1,0:T(8,128)(2,1)S(1)} collective-permute-done((bf16[80,896]{1,0:T(8,128)(2,1)S(1)}, bf16[80,896]{1,0:T(8,128)(2,1)S(1)}, u32[]{:S(2)}, u32[]{:S(2)}) %collective-permute-start.1) | collective-permute-done | bytes 143392 | tf_op jit(solution)/shard_map/ppermute | solution.py:13
  34.7 1.9 %collective-permute-done = bf16[80,896]{1,0:T(8,128)(2,1)S(1)} collective-permute-done((bf16[80,896]{1,0:T(8,128)(2,1)S(1)}, bf16[80,896]{1,0:T(8,128)(2,1)S(1)}, u32[]{:S(2)}, u32[]{:S(2)}) %collective-permute-start) | collective-permute-done | bytes 143392 | tf_op jit(solution)/shard_map/ppermute | solution.py:13
  37.5 12.5 %all-gather.5.cloned.1.call-done = bf16[4,80,3584]{2,1,0:T(8,128)(2,1)} async-done(((bf16[4,80,896]{2,1,0:T(8,128)(2,1)}), bf16[4,80,3584]{2,1,0:T(8,128)(2,1)}) %all-gather.5.cloned.1.call-update) | async-done | bytes 2293776 | tf_op jit(solution)/shard_map/all_gather | solution.py:87
  50.0 3.1 %fusion.47 = f32[320,256]{1,0:T(8,128)S(1)} fusion(bf16[320,3584]{1,0:T(8,128)(2,1)} %bitcast.79, bf16[1,3584,256]{2,1,0:T(8,128)(2,1)} %param.14), kind=kOutput, calls=%fused_computation.112 | convolution fusion | flops 587202560 | bytes 4456448 | tf_op jit(solution)/shard_map/dot_general | solution.py:24
  54.2 21.1 %all-gather.3.cloned.1.call-done = bf16[4,80,3584]{2,1,0:T(8,128)(2,1)} async-done(((bf16[4,80,896]{2,1,0:T(8,128)(2,1)}), bf16[4,80,3584]{2,1,0:T(8,128)(2,1)}) %all-gather.3.cloned.1.call-update) | async-done | bytes 2293776 | tf_op jit(solution)/shard_map/all_gather | solution.py:88
  75.3 2.7 %multiply_reduce_fusion = (f32[320]{0:T(512)S(1)}, bf16[320,256]{1,0:T(8,128)(2,1)S(1)}, bf16[320,256]{1,0:T(8,128)(2,1)S(1)}) fusion(f32[320,256]{1,0:T(8,128)S(1)} %fusion.47, f32[320,256]{1,0:T(8,128)S(1)} %fusion.45, bf16[320,3584]{1,0:T(8,128)(2,1)} %bitcast.81, bf16[1,256,3584]{2,1,0:T(8,128)(2,1)S(1)} %copy-done), kind=kOutput, calls=%fused_computation.37 | convolution fusion | flops 588512960 | bytes 5113088 | tf_op jit(solution)/shard_map/dot_general | solution.py:25
  78.1 3.5 %fusion = f32[320,3584]{1,0:T(8,128)} fusion(bf16[3584,256]{1,0:T(8,128)(2,1)S(1)} %bitcast.82, bf16[3584,256]{1,0:T(8,128)(2,1)S(1)} %bitcast.83, bf16[320,256]{1,0:T(8,128)(2,1)S(1)} %get-tuple-element.26, bf16[320,256]{1,0:T(8,128)(2,1)S(1)} %get-tuple-element.25), kind=kOutput, calls=%fused_computation.8 | convolution fusion | flops 1182400512 | bytes 8585216 | tf_op jit(solution)/shard_map/dot_general | solution.py:97
  83.0 6.1 %all-reduce = f32[4,80,4]{1,0,2:T(4,128)S(1)} all-reduce(f32[4,80,4]{1,0,2:T(4,128)S(1)} %broadcast_in_dim.72), channel_id=3, replica_groups=mesh['node'=8,'local'=4] {'local'}, use_global_device_ids=true, to_apply=%region_14.16.clone | all-reduce | flops 1280 | bytes 10240
  90.9 1.5 collective-permute-start.9
  93.6 1.6 collective-permute-done.11
  98.9 29.8 %reduce-scatter.2.cloned.1.call-done = f32[4,80,896]{2,1,0:T(8,128)} async-done(((f32[4,80,3584]{2,1,0:T(8,128)}), f32[4,80,896]{2,1,0:T(8,128)}) %reduce-scatter.2.cloned.1.call-update) | async-done | bytes 1146896 | tf_op jit(solution)/shard_map/reduce_scatter | solution.py:102
  128.7 2.2 %slice_bitcast_fusion.3 = (f32[80,896]{1,0:T(8,128)S(1)}, f32[80,896]{1,0:T(8,128)}, f32[80,896]{1,0:T(8,128)}, f32[80,896]{1,0:T(8,128)}) fusion(f32[4,80,896]{2,1,0:T(8,128)} %reduce-scatter.2.cloned.1.call-done), kind=kLoop, calls=%fused_computation.45 | loop fusion | bytes 2293760 | tf_op jit(solution)/shard_map/squeeze;stack;squeeze | solution.py:116
  131.9 1.4 collective-permute-start.6
  134.7 25.1 %collective-permute-done.8 = f32[80,896]{1,0:T(8,128)S(1)} collective-permute-done((f32[80,896]{1,0:T(8,128)}, f32[80,896]{1,0:T(8,128)S(1)}, u32[]{:S(2)}, u32[]{:S(2)}) %collective-permute-start.8) | collective-permute-done | bytes 286752 | tf_op jit(solution)/shard_map/ppermute | solution.py:13
  159.8 1.6 gather_fusion.3
  161.4 1.6 gather_fusion.2
  163.0 1.6 gather_fusion.1
  164.6 2.1 %fusion.9 = bf16[128,896]{1,0:T(8,128)(2,1)} fusion(f32[128,896]{1,0:T(8,128)S(1)} %copy-done.3, f32[128,896]{1,0:T(8,128)} %gather_fusion.2, f32[128,896]{1,0:T(8,128)} %gather_fusion.1, f32[128,896]{1,0:T(8,128)S(1)} %gather_fusion, f32[128]{0:T(128)S(1)} %get-tuple-element.7, f32[128]{0:T(128)S(1)} %get-tuple-element.6, f32[128]{0:T(128)S(1)} %get-tuple-element.5, ...), kind=kLoop, calls=%fused_computation.28 | loop fusion | flops 1376256 | bytes 2066944 | tf_op jit(solution)/shard_map/convert_element_type | solution.py:120
  (89 shorter events, 21.1 us)
Async XLA Ops:
  7.2 68.2 %copy-start = (bf16[1,256,3584]{2,1,0:T(8,128)(2,1)S(1)}, bf16[1,256,3584]{2,1,0:T(8,128)(2,1)}, u32[]{:S(2)}) copy-start(bf16[1,256,3584]{2,1,0:T(8,128)(2,1)} %param.15) | copy-start | bytes 5505028
  7.2 10.3 %copy-start.1 = (bf16[128,896]{1,0:T(8,128)(2,1)S(1)}, bf16[128,896]{1,0:T(8,128)(2,1)}, u32[]{:S(2)}) copy-start(bf16[128,896]{1,0:T(8,128)(2,1)} %param.11) | copy-start | bytes 688132
  7.2 14.5 %copy-start.2 = (bf16[128,896]{1,0:T(8,128)(2,1)S(1)}, bf16[128,896]{1,0:T(8,128)(2,1)}, u32[]{:S(2)}) copy-start(bf16[128,896]{1,0:T(8,128)(2,1)} %param.12) | copy-start | bytes 688132
  7.2 42.8 %all-gather.5.cloned.1.call-start = ((), (), s32[]{:S(2)}) async-start(), calls=%async_computation.2 | async-start | bytes 2867200 | tf_op jit(solution)/shard_map/all_gather | solution.py:87
  9.6 8.1 %collective-permute-start.5 = (bf16[80,896]{1,0:T(8,128)(2,1)S(1)}, bf16[80,896]{1,0:T(8,128)(2,1)S(1)}, u32[]{:S(2)}, u32[]{:S(2)}) collective-permute-start(bf16[80,896]{1,0:T(8,128)(2,1)S(1)} %convolution_convert_fusion), channel_id=1, source_target_pairs={{0,12},{4,16},{8,20},{12,24},{16,28},{20,0},{24,4},{28,8},{1,13},{... | collective-permute-start | bytes 430088 | tf_op jit(solution)/shard_map/ppermute | solution.py:13
  11.5 8.9 %collective-permute-start.4 = (bf16[80,896]{1,0:T(8,128)(2,1)S(1)}, bf16[80,896]{1,0:T(8,128)(2,1)S(1)}, u32[]{:S(2)}, u32[]{:S(2)}) collective-permute-start(bf16[80,896]{1,0:T(8,128)(2,1)S(1)} %convolution_convert_fusion.1), channel_id=1, source_target_pairs={{0,8},{4,12},{8,16},{12,20},{16,24},{20,28},{24,0},{28,4},{1,9},{5... | collective-permute-start | bytes 430088 | tf_op jit(solution)/shard_map/ppermute | solution.py:13
  15.6 5.2 %collective-permute-start.3 = (bf16[80,896]{1,0:T(8,128)(2,1)S(1)}, bf16[80,896]{1,0:T(8,128)(2,1)S(1)}, u32[]{:S(2)}, u32[]{:S(2)}) collective-permute-start(bf16[80,896]{1,0:T(8,128)(2,1)S(1)} %convolution_convert_fusion.2), channel_id=1, source_target_pairs={{0,4},{4,8},{8,12},{12,16},{16,20},{20,24},{24,28},{28,0},{1,5},{5... | collective-permute-start | bytes 430088 | tf_op jit(solution)/shard_map/ppermute | solution.py:13
  21.7 53.7 %all-gather.3.cloned.1.call-start = ((), (), s32[]{:S(2)}) async-start(), calls=%async_computation.1 | async-start | bytes 2867200 | tf_op jit(solution)/shard_map/all_gather | solution.py:88
  21.9 10.5 %collective-permute-start.2 = (bf16[80,896]{1,0:T(8,128)(2,1)S(1)}, bf16[80,896]{1,0:T(8,128)(2,1)S(1)}, u32[]{:S(2)}, u32[]{:S(2)}) collective-permute-start(bf16[80,896]{1,0:T(8,128)(2,1)S(1)} %convolution_convert_fusion.4), channel_id=1, source_target_pairs={{0,12},{4,16},{8,20},{12,24},{16,28},{20,0},{24,4},{28,8},{1,13},{... | collective-permute-start | bytes 430088 | tf_op jit(solution)/shard_map/ppermute | solution.py:13
  25.0 9.7 %collective-permute-start.1 = (bf16[80,896]{1,0:T(8,128)(2,1)S(1)}, bf16[80,896]{1,0:T(8,128)(2,1)S(1)}, u32[]{:S(2)}, u32[]{:S(2)}) collective-permute-start(bf16[80,896]{1,0:T(8,128)(2,1)S(1)} %convolution_convert_fusion.5), channel_id=1, source_target_pairs={{0,8},{4,12},{8,16},{12,20},{16,24},{20,28},{24,0},{28,4},{1,9},{5... | collective-permute-start | bytes 430088 | tf_op jit(solution)/shard_map/ppermute | solution.py:13
  30.7 5.9 %collective-permute-start = (bf16[80,896]{1,0:T(8,128)(2,1)S(1)}, bf16[80,896]{1,0:T(8,128)(2,1)S(1)}, u32[]{:S(2)}, u32[]{:S(2)}) collective-permute-start(bf16[80,896]{1,0:T(8,128)(2,1)S(1)} %convolution_convert_fusion.6), channel_id=1, source_target_pairs={{0,4},{4,8},{8,12},{12,16},{16,20},{20,24},{24,28},{28,0},{1,5},{5... | collective-permute-start | bytes 430088 | tf_op jit(solution)/shard_map/ppermute | solution.py:13
  37.5 91.2 %reduce-scatter.2.cloned.1.call-start = ((), (), s32[]{:S(2)}) async-start(), calls=%async_computation.3 | async-start | bytes 5734400 | tf_op jit(solution)/shard_map/reduce_scatter | solution.py:102
  50.0 3.1 %copy-start.6 = (bf16[4,80,3584]{2,1,0:T(8,128)(2,1)S(1)}, bf16[4,80,3584]{2,1,0:T(8,128)(2,1)}, u32[]{:S(2)}) copy-start(bf16[4,80,3584]{2,1,0:T(8,128)(2,1)} %all-gather.5.cloned.1.call-done) | copy-start | bytes 6881284
  50.0 3.4 %copy-start.8 = (bf16[1,3584,256]{2,1,0:T(8,128)(2,1)S(1)}, bf16[1,3584,256]{2,1,0:T(8,128)(2,1)}, u32[]{:S(2)}) copy-start(bf16[1,3584,256]{2,1,0:T(8,128)(2,1)} %param.13) | copy-start | bytes 5505028
  75.3 2.7 %copy-start.7 = (bf16[1,3584,256]{2,1,0:T(8,128)(2,1)S(1)}, bf16[1,3584,256]{2,1,0:T(8,128)(2,1)}, u32[]{:S(2)}) copy-start(bf16[1,3584,256]{2,1,0:T(8,128)(2,1)} %param.14) | copy-start | bytes 5505028
  75.3 2.7 %copy-start.9 = (bf16[1,3584,256]{2,1,0:T(8,128)(2,1)S(1)}, bf16[1,3584,256]{2,1,0:T(8,128)(2,1)}, u32[]{:S(2)}) copy-start(bf16[1,3584,256]{2,1,0:T(8,128)(2,1)} %param.13) | copy-start | bytes 5505028
  81.5 51.8 %copy-start.4 = (s32[128,2]{0,1:T(2,128)S(1)}, s32[128,2]{0,1:T(2,128)}, u32[]{:S(2)}) copy-start(s32[128,2]{0,1:T(2,128)} %param.16) | copy-start | bytes 3076
  81.6 51.8 %copy-start.5 = (s32[128,2]{0,1:T(2,128)S(1)}, s32[128,2]{0,1:T(2,128)}, u32[]{:S(2)}) copy-start(s32[128,2]{0,1:T(2,128)} %param.17) | copy-start | bytes 3076
  89.8 5.4 %collective-permute-start.11 = (f32[80,1]{0,1:T(1,128)S(1)}, f32[80,1]{0,1:T(1,128)S(1)}, u32[]{:S(2)}, u32[]{:S(2)}) collective-permute-start(f32[80,1]{0,1:T(1,128)S(1)} %get-tuple-element.28), channel_id=1, source_target_pairs={{0,20},{4,24},{8,28},{12,0},{16,4},{20,8},{24,12},{28,16},{1,21},{... | collective-permute-start | bytes 968 | tf_op jit(solution)/shard_map/ppermute | solution.py:13
  90.4 6.0 %collective-permute-start.10 = (f32[80,1]{0,1:T(1,128)S(1)}, f32[80,1]{0,1:T(1,128)S(1)}, u32[]{:S(2)}, u32[]{:S(2)}) collective-permute-start(f32[80,1]{0,1:T(1,128)S(1)} %get-tuple-element.29), channel_id=1, source_target_pairs={{0,24},{4,28},{8,0},{12,4},{16,8},{20,12},{24,16},{28,20},{1,25},{... | collective-permute-start | bytes 968 | tf_op jit(solution)/shard_map/ppermute | solution.py:13
  90.9 6.7 %collective-permute-start.9 = (f32[80,1]{0,1:T(1,128)S(1)}, f32[80,1]{0,1:T(1,128)S(1)}, u32[]{:S(2)}, u32[]{:S(2)}) collective-permute-start(f32[80,1]{0,1:T(1,128)S(1)} %get-tuple-element.30), channel_id=1, source_target_pairs={{0,28},{4,0},{8,4},{12,8},{16,12},{20,16},{24,20},{28,24},{1,29},{... | collective-permute-start | bytes 968 | tf_op jit(solution)/shard_map/ppermute | solution.py:13
  130.8 29.0 %collective-permute-start.8 = (f32[80,896]{1,0:T(8,128)}, f32[80,896]{1,0:T(8,128)S(1)}, u32[]{:S(2)}, u32[]{:S(2)}) collective-permute-start(f32[80,896]{1,0:T(8,128)} %get-tuple-element.21), channel_id=1, source_target_pairs={{0,20},{4,24},{8,28},{12,0},{16,4},{20,8},{24,12},{28,16},{1,21},{... | collective-permute-start | bytes 860168 | tf_op jit(solution)/shard_map/ppermute | solution.py:13
  131.4 30.1 %collective-permute-start.7 = (f32[80,896]{1,0:T(8,128)}, f32[80,896]{1,0:T(8,128)S(1)}, u32[]{:S(2)}, u32[]{:S(2)}) collective-permute-start(f32[80,896]{1,0:T(8,128)} %get-tuple-element.22), channel_id=1, source_target_pairs={{0,24},{4,28},{8,0},{12,4},{16,8},{20,12},{24,16},{28,20},{1,25},{... | collective-permute-start | bytes 860168 | tf_op jit(solution)/shard_map/ppermute | solution.py:13
  131.9 31.1 %collective-permute-start.6 = (f32[80,896]{1,0:T(8,128)}, f32[80,896]{1,0:T(8,128)S(1)}, u32[]{:S(2)}, u32[]{:S(2)}) collective-permute-start(f32[80,896]{1,0:T(8,128)} %get-tuple-element.23), channel_id=1, source_target_pairs={{0,28},{4,0},{8,4},{12,8},{16,12},{20,16},{24,20},{28,24},{1,29},{... | collective-permute-start | bytes 860168 | tf_op jit(solution)/shard_map/ppermute | solution.py:13
  (2 other events, 2.2 us)
Sparse Core Ops, SparseCore 0:
  21.8 28.2 all-gather.4
  51.6 23.6 all-gather.2
  81.7 46.9 reduce-scatter.1
where the time goes:
time: 174 us; the launch traced here: 173 us
  waiting for transfers between devices  98.7 us (57%)
  starting transfers between devices  18.1 us (10%)
  local copies, waits for them, and re-layouts  15.4 us (9%)
  matrix products  14.3 us (8%)
  between operations  14.1 us (8%)
  other arithmetic  6.52 us (4%)
  blocking collectives  6.14 us (4%)
    ppermute x12, waiting for transfers between devices, from_behind(): return lax.ppermute(value, axis, pairs)  35.3 us
    reduce_scatter x1, waiting for transfers between devices, body(): lax.psum_scatter(back.reshape(GROUP, CAPACITY, width), 'local', scatter_d...  29.8 us
    all_gather x1, waiting for transfers between devices, body(): lax.all_gather(got_grad, 'local', axis=2, tiled=True)  21.1 us
    ppermute x12, starting transfers between devices, from_behind(): return lax.ppermute(value, axis, pairs)  18 us
    all_gather x1, waiting for transfers between devices, body(): lax.all_gather(got_in, 'local', axis=2, tiled=True)  12.5 us
    unnamed x1, blocking collectives  6.14 us
    gather x4, local copies, waits for them, and re-layouts, body(): rows_back = jnp.take(home_back[offset], slot_list[offset], axis=0)  5.57 us
    gather x4, local copies, waits for them, and re-layouts, body(): gate_back = jnp.take(home_gate[offset], slot_list[offset], axis=0)  4.9 us
  transfers between devices with their start and end apart: 15, of which 10 were waited for; matrix products, arithmetic and copies ran while one was open for 12% of the time, Pallas kernels for 0%

commit v1 on v0

v1 whole, which is shorter than its diff:
```python
import functools

import jax
import jax.numpy as jnp
from jax import lax
from jax.experimental import pallas as pl
from jax.experimental.pallas import tpu as pltpu
from jax.sharding import PartitionSpec as P

GROUP = 4
CAPACITY = 80
LANES = 128
MESH = pl.DeviceIdType.MESH
NT = (((1,), (1,)), ((), ()))
TN = (((0,), (0,)), ((), ()))


def dot(a, b, dims=None):
    if dims is None:
        return jnp.dot(a, b, preferred_element_type=jnp.float32)
    return lax.dot_general(a, b, dims, preferred_element_type=jnp.float32)


def lane_index(rows):
    return lax.broadcasted_iota(jnp.int32, (rows, LANES), 1)


def split_gate(value):
    high = value.astype(jnp.bfloat16).astype(jnp.float32)
    low = value - high
    return jnp.where(lane_index(value.shape[0]) < LANES // 2, high, low).astype(jnp.bfloat16)


def join_gate(parts):
    lanes = lane_index(parts.shape[0])
    keep = (lanes == 0) | (lanes == LANES // 2)
    return jnp.sum(jnp.where(keep, parts.astype(jnp.float32), 0.0), axis=1, keepdims=True)


def kernel(
    nodes, locals_,
    x_ref, g_ref, gate_hbm, up_hbm, down_hbm, route_ref, fixed_ref,
    out_ref, ggrad_ref,
    gw, uw, dw, table, packed, got, out_a, in_a, own, own_gate, out_b, in_b, mine, out_h, in_h,
    wsem, ns, nr, hs, hr, ls, lr, sa, ra, sb, rb, sm, rm,
):
    tokens, feat = x_ref.shape
    wide = out_h.shape[2]
    gate_lanes = pl.ds(wide - LANES, LANES)
    his = locals_ // 2
    node, me = lax.axis_index("node"), lax.axis_index("local")
    hi, lo = me // 2, me % 2
    mate = hi * 2 + (1 - lo)

    def ahead(steps):
        return (lax.rem(node + steps + nodes, nodes), me)

    def beside(index):
        return (node, index)

    def turned(d):
        return lax.rem(hi + d, his)

    weights = [
        pltpu.make_async_copy(source.at[0], dest, wsem.at[i])
        for i, (source, dest) in enumerate(((gate_hbm, gw), (up_hbm, uw), (down_hbm, dw)))
    ]
    for copy in weights:
        copy.start()

    barrier = pltpu.get_barrier_semaphore()
    friends = [ahead(s) for o in range(1, GROUP) for s in (o, -o)]
    friends += [beside(turned(d) * 2 + lo) for d in range(1, his)]
    friends += [beside(mate)]
    for friend in friends:
        pl.semaphore_signal(barrier, inc=1, device_id=friend, device_id_type=MESH)

    def remote(source, dest, send, recv, device):
        return pltpu.make_async_remote_copy(
            src_ref=source, dst_ref=dest, send_sem=send, recv_sem=recv,
            device_id=device, device_id_type=MESH,
        )

    def to_node(o, k):
        return remote(packed.at[o, k], got.at[o, me, k], ns.at[o, k], nr.at[o, k], ahead(o))

    def to_hi(o, k, d):
        return remote(
            got.at[o, me, k], got.at[o, me, k], hs.at[o, k, d], hr.at[o, k, hi],
            beside(turned(d) * 2 + lo),
        )

    def from_hi(o, k, d):
        h = turned(d)
        slot = got.at[o, h * 2 + lo, k]
        return remote(slot, slot, hs.at[o, k, d], hr.at[o, k, h], beside(h * 2 + lo))

    def to_mate(o, k, h):
        slot = got.at[o, h * 2 + lo, k]
        return remote(slot, slot, ls.at[o, k, h], lr.at[o, k, h], beside(mate))

    def from_mate(o, k, h):
        slot = got.at[o, h * 2 + 1 - lo, k]
        return remote(slot, slot, ls.at[o, k, h], lr.at[o, k, h], beside(mate))

    def sum_mate(o):
        return remote(out_a.at[o], in_a.at[o], sa.at[o], ra.at[o], beside(mate))

    def sum_hi(o, d):
        h = turned(d)
        return remote(out_b.at[o, h], in_b.at[o, hi], sb.at[o, h], rb.at[o, hi], beside(h * 2 + lo))

    def sum_from_hi(o, d):
        h = turned(d)
        return remote(out_b.at[o, h], in_b.at[o, h], sb.at[o, h], rb.at[o, h], beside(h * 2 + lo))

    def to_home(o):
        return remote(out_h.at[o], in_h.at[o], sm.at[o], rm.at[o], ahead(-o))

    route = route_ref[...]
    lanes = lane_index(tokens)
    chosen = ((route[:, 0:1] == lanes) | (route[:, 1:2] == lanes)).astype(jnp.float32)
    row = lax.broadcasted_iota(jnp.int32, (tokens, tokens), 0)
    column = lax.broadcasted_iota(jnp.int32, (tokens, tokens), 1)
    below = (column <= row).astype(jnp.float32).astype(jnp.bfloat16)
    ranks = dot(below, chosen.astype(jnp.bfloat16))
    slots = lax.broadcasted_iota(jnp.int32, (tokens, CAPACITY), 1).astype(jnp.float32) + 1.0
    tables = []
    for o in range(GROUP):
        here = (ranks[:, o:o + 1] == slots) & (chosen[:, o:o + 1] > 0.5)
        tables.append(here.astype(jnp.float32).astype(jnp.bfloat16))
        table[o] = tables[o]

    def pack(o, k):
        source = x_ref if k == 0 else g_ref
        return dot(tables[o], source[...], TN).astype(jnp.bfloat16)

    for k in range(2):
        got[0, me, k] = pack(0, k)
    pl.semaphore_wait(barrier, len(friends))
    for k in range(2):
        for d in range(1, his):
            to_hi(0, k, d).start()
    for o in range(1, GROUP):
        for k in range(2):
            packed[o, k] = pack(o, k)
            to_node(o, k).start()
    for k in range(2):
        to_mate(0, k, hi).start()
    for copy in weights:
        copy.wait()

    def spread(o):
        for k in range(2):
            to_node(o, k).wait_recv()
            for d in range(1, his):
                to_hi(o, k, d).start()
            to_mate(o, k, hi).start()

    def pass_on(o):
        for k in range(2):
            for d in range(1, his):
                from_hi(o, k, d).wait_recv()
                to_mate(o, k, turned(d)).start()

    def compute(o):
        for k in range(2):
            for h in range(his):
                from_mate(o, k, h).wait_recv()
        a = b = v = None
        for l in range(locals_):
            rows = pl.ds(l * feat, feat)
            x, g = got[o, l, 0], got[o, l, 1]
            pa, pb, pv = dot(x, gw[rows, :]), dot(x, uw[rows, :]), dot(g, dw[:, rows], NT)
            a, b, v = (pa, pb, pv) if a is None else (a + pa, b + pb, v + pv)
        s = 1.0 / (1.0 + jnp.exp(-a))
        swish = a * s
        part = split_gate(jnp.sum(swish * b * v, axis=1, keepdims=True))
        u = (v * swish).astype(jnp.bfloat16)
        w = (v * b * s * (1.0 + a * (1.0 - s))).astype(jnp.bfloat16)

        def back(l):
            rows = pl.ds(pl.multiple_of(l * feat, 64), feat)
            return dot(w, gw[rows, :], NT) + dot(u, uw[rows, :], NT)

        for h in range(his):
            out_a[o, h, :, pl.ds(0, feat)] = back(h * 2 + 1 - lo).astype(jnp.bfloat16)
            out_a[o, h, :, gate_lanes] = part
        sum_mate(o).start()
        own_gate[...] = part
        for h in range(his):
            own[h] = back(h * 2 + lo)

    def add_mate(o):
        sum_mate(o).wait_recv()
        gate = split_gate(join_gate(own_gate[...]) + join_gate(in_a[o, 0, :, gate_lanes]))
        for d in range(1, his):
            h = turned(d)
            total = own[h] + in_a[o, h, :, pl.ds(0, feat)].astype(jnp.float32)
            out_b[o, h, :, pl.ds(0, feat)] = total.astype(jnp.bfloat16)
            out_b[o, h, :, gate_lanes] = gate
            sum_hi(o, d).start()
        mine[o] = own[hi] + in_a[o, hi, :, pl.ds(0, feat)].astype(jnp.float32)
        in_b[o, hi, :, gate_lanes] = gate

    def add_hi(o):
        total = mine[o]
        for d in range(1, his):
            sum_from_hi(o, d).wait_recv()
            total = total + in_b[o, turned(d), :, pl.ds(0, feat)].astype(jnp.float32)
        gate = join_gate(in_b[o, 0, :, gate_lanes])
        for h in range(1, his):
            gate = gate + join_gate(in_b[o, h, :, gate_lanes])
        out_h[o, :, pl.ds(0, feat)] = total.astype(jnp.bfloat16)
        out_h[o, :, gate_lanes] = split_gate(gate)

        @pl.when(o > 0)
        def _():
            to_home(o).start()

    def step(i, carry):
        @pl.when(i + 1 < GROUP)
        def _():
            spread(i + 1)

        @pl.when(i < GROUP)
        def _():
            pass_on(i)

        @pl.when((i >= 1) & (i <= GROUP))
        def _():
            add_mate(i - 1)

        @pl.when(i >= 2)
        def _():
            add_hi(i - 2)

        @pl.when(i < GROUP)
        def _():
            compute(i)

        return carry

    lax.fori_loop(0, GROUP + 2, step, 0)

    gates = fixed_ref[...].astype(jnp.float32) / 65536.0
    total = jnp.zeros((tokens, feat), jnp.float32)
    gate_total = jnp.zeros(gates.shape, jnp.float32)
    for o in range(GROUP):
        if o > 0:
            to_home(o).wait_recv()
        home = out_h if o == 0 else in_h
        hits = route == o
        weight = jnp.sum(jnp.where(hits, gates, 0.0), axis=1, keepdims=True)
        total = total + weight * dot(table[o], home[o, :, pl.ds(0, feat)])
        back_gate = join_gate(dot(table[o], home[o, :, gate_lanes]))
        gate_total = gate_total + jnp.where(hits, back_gate, 0.0)
    out_ref[...] = total.astype(jnp.bfloat16)
    ggrad_ref[...] = gate_total

    def finish(o, carry):
        for k in range(2):
            for d in range(1, his):
                to_hi(o, k, d).wait_send()
            for h in range(his):
                to_mate(o, k, h).wait_send()
        sum_mate(o).wait_send()
        for d in range(1, his):
            sum_hi(o, d).wait_send()

        @pl.when(o > 0)
        def _():
            for k in range(2):
                to_node(o, k).wait_send()
            to_home(o).wait_send()

        return carry

    lax.fori_loop(0, GROUP, finish, 0)


def body(nodes, locals_, layer_input, output_grad, gate_weight, up_weight, down_weight, route, fixed):
    tokens, feat = layer_input.shape
    width, hidden = gate_weight.shape[1:]
    his = locals_ // 2
    wide = -(-feat // LANES) * LANES + LANES
    bf16, f32 = jnp.bfloat16, jnp.float32
    vmem, dma = pltpu.VMEM, pltpu.SemaphoreType.DMA
    scratch = [
        vmem((width, hidden), bf16),
        vmem((width, hidden), bf16),
        vmem((hidden, width), bf16),
        vmem((GROUP, tokens, CAPACITY), bf16),
        vmem((GROUP, 2, CAPACITY, feat), bf16),
        vmem((GROUP, locals_, 2, CAPACITY, feat), bf16),
        vmem((GROUP, his, CAPACITY, wide), bf16),
        vmem((GROUP, his, CAPACITY, wide), bf16),
        vmem((his, CAPACITY, feat), f32),
        vmem((CAPACITY, LANES), bf16),
        vmem((GROUP, his, CAPACITY, wide), bf16),
        vmem((GROUP, his, CAPACITY, wide), bf16),
        vmem((GROUP, CAPACITY, feat), f32),
        vmem((GROUP, CAPACITY, wide), bf16),
        vmem((GROUP, CAPACITY, wide), bf16),
        dma((3,)),
        dma((GROUP, 2)),
        dma((GROUP, 2)),
        dma((GROUP, 2, his)),
        dma((GROUP, 2, his)),
        dma((GROUP, 2, his)),
        dma((GROUP, 2, his)),
        dma((GROUP,)),
        dma((GROUP,)),
        dma((GROUP, his)),
        dma((GROUP, his)),
        dma((GROUP,)),
        dma((GROUP,)),
    ]
    in_vmem, anywhere = pl.BlockSpec(memory_space=pltpu.VMEM), pl.BlockSpec(memory_space=pl.ANY)
    routed = GROUP * CAPACITY
    return pl.pallas_call(
        functools.partial(kernel, nodes, locals_),
        out_shape=(
            jax.ShapeDtypeStruct((tokens, feat), bf16),
            jax.ShapeDtypeStruct(fixed.shape, f32),
        ),
        in_specs=[in_vmem, in_vmem, anywhere, anywhere, anywhere, in_vmem, in_vmem],
        out_specs=(in_vmem, in_vmem),
        scratch_shapes=scratch,
        compiler_params=pltpu.CompilerParams(
            collective_id=0, has_side_effects=True, vmem_limit_bytes=48 * 1024 * 1024
        ),
        cost_estimate=pl.CostEstimate(
            flops=10 * routed * width * hidden,
            bytes_accessed=6 * width * hidden + 6 * tokens * feat,
            transcendentals=routed * hidden,
        ),
    )(layer_input, output_grad, gate_weight, up_weight, down_weight, route, fixed)


def solution(mesh):
    in_specs = (
        P("node", "local"),
        P("node", "local"),
        P("node", None, "local"),
        P("node", None, "local"),
        P("node", "local", None),
        P("node", None),
        P("node", None),
    )
    out_specs = (P("node", "local"), P("node", None))
    run = functools.partial(body, mesh.shape["node"], mesh.shape["local"])
    return jax.shard_map(run, mesh=mesh, in_specs=in_specs, out_specs=out_specs, check_vma=False)
```

time: 174 us -> 66.8 us (0.38)
  waiting for transfers between devices: 98.7 us -> 0 us
  Pallas kernels: 0 us -> 58.1 us
  starting transfers between devices: 18.1 us -> 0 us
  matrix products: 14.3 us -> 0 us
  between operations: 14.1 us -> 0.65 us
  local copies, waits for them, and re-layouts: 15.4 us -> 7.76 us
  other arithmetic: 6.52 us -> 0 us
  blocking collectives: 6.14 us -> 0 us
    pallas_call x0 -> x1, Pallas kernels: none -> 58.1 us  [body(): pl.pallas_call(functools.partial(kernel, nodes, locals_), out_shape=(jax....]
    ppermute x12 -> x0, waiting for transfers between devices: 35.3 us -> none  [from_behind(): return lax.ppermute(value, axis, pairs)]
    all_gather x2 -> x0, waiting for transfers between devices: 33.6 us -> none  [the longest x1 21.1 us: body(): lax.all_gather(got_grad, 'local', axis=2, tiled=True)]
    reduce_scatter x1 -> x0, waiting for transfers between devices: 29.8 us -> none  [body(): lax.psum_scatter(back.reshape(GROUP, CAPACITY, width), 'local', scatter_d...]
    ppermute x12 -> x0, starting transfers between devices: 18 us -> none  [from_behind(): return lax.ppermute(value, axis, pairs)]
    dot_general x12 -> x0, matrix products: 14.3 us -> none  [the longest x4 3.58 us: body(): jnp.dot(table, layer_input, preferred_element_type=jnp.float32)]
    gather x8 -> x0, local copies, waits for them, and re-layouts: 10.5 us -> none  [the longest x4 5.57 us: body(): rows_back = jnp.take(home_back[offset], slot_list[offset], axis=0)]
    unnamed x1 -> x0, blocking collectives: 6.14 us -> none
  transfers between devices with their start and end apart: 15 -> 0, of which waited for: 10 -> 0; matrix products, arithmetic and copies ran while one was open for 12% -> 0% of each run, Pallas kernels for 0% -> 0%
where the time goes in v1:
time: 66.8 us; the launch traced here: 66.5 us
  Pallas kernels  58.1 us (87%)
  local copies, waits for them, and re-layouts  7.76 us (12%)
    pallas_call x1, Pallas kernels, body(): pl.pallas_call(functools.partial(kernel, nodes, locals_), out_shape=(jax....  58.1 us
    unnamed x11, local copies, waits for them, and re-layouts  7.13 us

profile of v1, /device:TPU:26, one launch (start us, length us, event | category | flops | bytes accessed | tf_op | source)
XLA Modules:
  0.0 66.5 jit_solution(11807501796981169044)
XLA Ops:
  0.6 0.8 %copy.9.route_ref = s32[128,2]{1,0:T(8,128)S(1)} copy(s32[128,2]{0,1:T(2,128)} %param.12) | data formatting | bytes 2048 | tf_op args[5]
  1.4 0.8 %copy.10.fixed_ref = s32[128,2]{1,0:T(8,128)S(1)} copy(s32[128,2]{0,1:T(2,128)} %param.13) | data formatting | bytes 2048 | tf_op args[6]
  2.2 0.0 copy-start
  2.2 1.5 %copy-done = bf16[1,3584,256]{2,1,0:T(8,128)(2,1)S(1)} copy-done((bf16[1,3584,256]{2,1,0:T(8,128)(2,1)S(1)}, bf16[1,3584,256]{2,1,0:T(8,128)(2,1)}, u32[]{:S(2)}) %copy-start) | copy-done | bytes 1835032
  3.7 0.0 copy-start.1
  3.7 1.5 %copy-done.1 = bf16[1,3584,256]{2,1,0:T(8,128)(2,1)S(1)} copy-done((bf16[1,3584,256]{2,1,0:T(8,128)(2,1)S(1)}, bf16[1,3584,256]{2,1,0:T(8,128)(2,1)}, u32[]{:S(2)}) %copy-start.1) | copy-done | bytes 1835032
  5.2 0.0 copy-start.2
  5.2 0.9 %copy-done.2 = bf16[128,896]{1,0:T(8,128)(2,1)S(1)} copy-done((bf16[128,896]{1,0:T(8,128)(2,1)S(1)}, bf16[128,896]{1,0:T(8,128)(2,1)}, u32[]{:S(2)}) %copy-start.2) | copy-done | bytes 229400
  6.1 0.0 copy-start.3
  6.1 0.9 %copy-done.3 = bf16[128,896]{1,0:T(8,128)(2,1)S(1)} copy-done((bf16[128,896]{1,0:T(8,128)(2,1)S(1)}, bf16[128,896]{1,0:T(8,128)(2,1)}, u32[]{:S(2)}) %copy-start.3) | copy-done | bytes 229400
  7.1 58.1 %shard_map.86 = (bf16[128,896]{1,0:T(8,128)(2,1)S(1)}, f32[128,2]{1,0:T(8,128)S(1)}) custom-call(bf16[128,896]{1,0:T(8,128)(2,1)S(1)} %copy-done.2, bf16[128,896]{1,0:T(8,128)(2,1)S(1)} %copy-done.3, bf16[1,3584,256]{2,1,0:T(8,128)(2,1)S(1)} %copy-done, bf16[1,3584,256]{2,1,0:T(8,128)(2,1)S(1)} %copy-done.1, bf16[1,256,3584]{2,1,0:T(8,128)(2,1)} %down_hbm.1, ...), custom_call_target="tpu_custom_call" | custom-call | flops 2936012800 | bytes 6193152 | tf_op jit(solution)/shard_map/pallas_call | solution.py:321
  65.2 0.6 copy.11
  65.9 0.7 %copy.13 = bf16[128,896]{1,0:T(8,128)(2,1)} copy(bf16[128,896]{1,0:T(8,128)(2,1)S(1)} %get-tuple-element.6) | data formatting | bytes 458752
Async XLA Ops:
  2.2 1.5 %copy-start = (bf16[1,3584,256]{2,1,0:T(8,128)(2,1)S(1)}, bf16[1,3584,256]{2,1,0:T(8,128)(2,1)}, u32[]{:S(2)}) copy-start(bf16[1,3584,256]{2,1,0:T(8,128)(2,1)} %gate_hbm.1) | copy-start | bytes 5505028
  3.7 1.5 %copy-start.1 = (bf16[1,3584,256]{2,1,0:T(8,128)(2,1)S(1)}, bf16[1,3584,256]{2,1,0:T(8,128)(2,1)}, u32[]{:S(2)}) copy-start(bf16[1,3584,256]{2,1,0:T(8,128)(2,1)} %up_hbm.1) | copy-start | bytes 5505028
  5.2 0.9 %copy-start.2 = (bf16[128,896]{1,0:T(8,128)(2,1)S(1)}, bf16[128,896]{1,0:T(8,128)(2,1)}, u32[]{:S(2)}) copy-start(bf16[128,896]{1,0:T(8,128)(2,1)} %x_ref.1) | copy-start | bytes 688132
  6.1 0.9 %copy-start.3 = (bf16[128,896]{1,0:T(8,128)(2,1)S(1)}, bf16[128,896]{1,0:T(8,128)(2,1)}, u32[]{:S(2)}) copy-start(bf16[128,896]{1,0:T(8,128)(2,1)} %g_ref.1) | copy-start | bytes 688132

commit v2 on v1

v2 whole, which is shorter than its diff:
```python
import functools

import jax
import jax.numpy as jnp
from jax import lax
from jax.experimental import pallas as pl
from jax.experimental.pallas import tpu as pltpu
from jax.sharding import PartitionSpec as P

GROUP = 4
CAPACITY = 80
LANES = 128
MESH = pl.DeviceIdType.MESH
NT = (((1,), (1,)), ((), ()))
TN = (((0,), (0,)), ((), ()))


def dot(a, b, dims=None):
    if dims is None:
        return jnp.dot(a, b, preferred_element_type=jnp.float32)
    return lax.dot_general(a, b, dims, preferred_element_type=jnp.float32)


def split_gate(value):
    high = value.astype(jnp.bfloat16).astype(jnp.float32)
    return jnp.concatenate((high, value - high), axis=0).astype(jnp.bfloat16)


def join_gate(parts):
    parts = parts.astype(jnp.float32)
    return parts[0:8] + parts[8:16]


def lay_down(column):
    wide = jnp.broadcast_to(column, (CAPACITY, LANES))
    rest = jnp.zeros((LANES - CAPACITY, LANES), jnp.float32)
    return jnp.concatenate((wide, rest), axis=0).T[0:8]


def stand_up(row):
    return jnp.broadcast_to(row, (LANES, row.shape[1])).T


def kernel(
    nodes, locals_,
    x_hbm, g_hbm, gate_hbm, up_hbm, down_hbm, route_hbm, fixed_hbm,
    out_ref, ggrad_ref,
    x_ref, g_ref, gw, uw, dw, route_ref, fixed_ref,
    table, packed, got, out_a, in_a, out_b, in_b, mine, out_h, in_h,
    gate_out_a, gate_in_a, gate_out_b, gate_in_b, gate_out_h, gate_in_h,
    wsem, ns, nr, hs, hr, ls, lr, sa, ra, sb, rb, sm, rm, sga, rga, sgb, rgb, sgm, rgm,
):
    tokens, feat = x_ref.shape
    his = locals_ // 2
    node, me = lax.axis_index("node"), lax.axis_index("local")
    hi, lo = me // 2, me % 2
    mate = hi * 2 + (1 - lo)

    def ahead(steps):
        return (lax.rem(node + steps + nodes, nodes), me)

    def beside(index):
        return (node, index)

    def turned(d):
        return lax.rem(hi + d, his)

    fetches = [
        pltpu.make_async_copy(source, dest, wsem.at[i])
        for i, (source, dest) in enumerate((
            (route_hbm, route_ref), (x_hbm, x_ref), (g_hbm, g_ref), (fixed_hbm, fixed_ref),
            (gate_hbm.at[0], gw), (up_hbm.at[0], uw), (down_hbm.at[0], dw),
        ))
    ]
    for copy in fetches:
        copy.start()

    barrier = pltpu.get_barrier_semaphore()
    friends = [ahead(s) for o in range(1, GROUP) for s in (o, -o)]
    friends += [beside(turned(d) * 2 + lo) for d in range(1, his)]
    friends += [beside(mate)]
    for friend in friends:
        pl.semaphore_signal(barrier, inc=1, device_id=friend, device_id_type=MESH)

    def remote(source, dest, send, recv, device):
        return pltpu.make_async_remote_copy(
            src_ref=source, dst_ref=dest, send_sem=send, recv_sem=recv,
            device_id=device, device_id_type=MESH,
        )

    def to_node(o, k):
        return remote(packed.at[o, k], got.at[o, me, k], ns.at[o, k], nr.at[o, k], ahead(o))

    def to_hi(o, k, d):
        return remote(
            got.at[o, me, k], got.at[o, me, k], hs.at[o, k, d], hr.at[o, k, hi],
            beside(turned(d) * 2 + lo),
        )

    def from_hi(o, k, d):
        h = turned(d)
        slot = got.at[o, h * 2 + lo, k]
        return remote(slot, slot, hs.at[o, k, d], hr.at[o, k, h], beside(h * 2 + lo))

    def to_mate(o, k, h):
        slot = got.at[o, h * 2 + lo, k]
        return remote(slot, slot, ls.at[o, k, h], lr.at[o, k, h], beside(mate))

    def from_mate(o, k, h):
        slot = got.at[o, h * 2 + 1 - lo, k]
        return remote(slot, slot, ls.at[o, k, h], lr.at[o, k, h], beside(mate))

    def sum_mate(o, h):
        return remote(out_a.at[o, h], in_a.at[o, h], sa.at[o, h], ra.at[o, h], beside(mate))

    def sum_hi(o, d):
        h = turned(d)
        return remote(out_b.at[o, h], in_b.at[o, hi], sb.at[o, h], rb.at[o, hi], beside(h * 2 + lo))

    def sum_from_hi(o, d):
        h = turned(d)
        return remote(out_b.at[o, h], in_b.at[o, h], sb.at[o, h], rb.at[o, h], beside(h * 2 + lo))

    def to_home(o):
        return remote(out_h.at[o], in_h.at[o], sm.at[o], rm.at[o], ahead(-o))

    def gate_mate(o):
        return remote(gate_out_a.at[o], gate_in_a.at[o], sga.at[o], rga.at[o], beside(mate))

    def gate_hi(o, d):
        h = turned(d)
        return remote(
            gate_out_b.at[o], gate_in_b.at[o, hi], sgb.at[o, h], rgb.at[o, hi], beside(h * 2 + lo)
        )

    def gate_from_hi(o, d):
        h = turned(d)
        return remote(
            gate_out_b.at[o], gate_in_b.at[o, h], sgb.at[o, h], rgb.at[o, h], beside(h * 2 + lo)
        )

    def gate_home(o):
        return remote(gate_out_h.at[o], gate_in_h.at[o], sgm.at[o], rgm.at[o], ahead(-o))

    fetches[0].wait()
    lanes = lax.broadcasted_iota(jnp.int32, (tokens, LANES), 1).astype(jnp.float32)
    routes = [stand_up(route_ref[k:k + 1, :].astype(jnp.float32)) for k in range(2)]
    chosen = ((routes[0] == lanes) | (routes[1] == lanes)).astype(jnp.float32)
    row = lax.broadcasted_iota(jnp.int32, (tokens, tokens), 0)
    column = lax.broadcasted_iota(jnp.int32, (tokens, tokens), 1)
    below = (column <= row).astype(jnp.float32).astype(jnp.bfloat16)
    ranks = dot(below, chosen.astype(jnp.bfloat16))
    slots = lax.broadcasted_iota(jnp.int32, (tokens, CAPACITY), 1).astype(jnp.float32) + 1.0
    tables = []
    for o in range(GROUP):
        here = (ranks[:, o:o + 1] == slots) & (chosen[:, o:o + 1] > 0.5)
        tables.append(here.astype(jnp.float32).astype(jnp.bfloat16))
        table[o] = tables[o]

    def pack(o, k):
        source = x_ref if k == 0 else g_ref
        return dot(tables[o], source[...], TN).astype(jnp.bfloat16)

    fetches[1].wait()
    got[0, me, 0] = pack(0, 0)
    packed[1, 0] = pack(1, 0)
    fetches[2].wait()
    pl.semaphore_wait(barrier, len(friends))
    for d in range(1, his):
        to_hi(0, 0, d).start()
    to_node(1, 0).start()
    got[0, me, 1] = pack(0, 1)
    for d in range(1, his):
        to_hi(0, 1, d).start()
    packed[1, 1] = pack(1, 1)
    to_node(1, 1).start()
    for o in range(2, GROUP):
        for k in range(2):
            packed[o, k] = pack(o, k)
            to_node(o, k).start()
    for k in range(2):
        to_mate(0, k, hi).start()
    for copy in fetches[3:]:
        copy.wait()

    def spread(o):
        for k in range(2):
            to_node(o, k).wait_recv()
            for d in range(1, his):
                to_hi(o, k, d).start()
            to_mate(o, k, hi).start()

    def block(l):
        return pl.ds(pl.multiple_of(l * feat, 64), feat)

    def arrivals(o, k, add):
        add(me)
        from_mate(o, k, hi).wait_recv()
        add(mate)
        for d in range(1, his):
            h = turned(d)
            from_hi(o, k, d).wait_recv()
            to_mate(o, k, h).start()
            add(h * 2 + lo)
            from_mate(o, k, h).wait_recv()
            add(h * 2 + 1 - lo)

    def compute(o):
        sums = [jnp.zeros((CAPACITY, gw.shape[1]), jnp.float32) for _ in range(3)]

        def add_input(l):
            x = got[o, l, 0]
            sums[0] = sums[0] + dot(x, gw[block(l), :])
            sums[1] = sums[1] + dot(x, uw[block(l), :])

        def add_grad(l):
            if feat % LANES == 0:
                rows = pl.ds(pl.multiple_of(l * feat, LANES), feat)
                sums[2] = sums[2] + dot(got[o, l, 1], dw[:, rows], NT)

        arrivals(o, 0, add_input)
        arrivals(o, 1, add_grad)
        if feat % LANES:
            for l in range(locals_):
                sums[2] = sums[2] + dot(got[o, l, 1], dw[:, pl.ds(l * feat, feat)], NT)
        a, b, v = sums
        s = 1.0 / (1.0 + jnp.exp(-a))
        swish = a * s
        u = (v * swish).astype(jnp.bfloat16)
        w = (v * b * s * (1.0 + a * (1.0 - s))).astype(jnp.bfloat16)
        gate_out_a[o] = split_gate(lay_down(jnp.sum(swish * b * v, axis=1, keepdims=True)))
        gate_mate(o).start()

        @pl.when(o >= 1)
        def _():
            add_hi(o - 1)

        def back(l):
            return dot(w, gw[block(l), :], NT) + dot(u, uw[block(l), :], NT)

        def send_mate(h):
            out_a[o, h] = back(h * 2 + 1 - lo).astype(jnp.bfloat16)
            sum_mate(o, h).start()

        def with_mate(h, part):
            sum_mate(o, h).wait_recv()
            return part + in_a[o, h].astype(jnp.float32)

        for d in range(1, his):
            send_mate(turned(d))
        parts = [back(turned(d) * 2 + lo) for d in range(1, his)]
        send_mate(hi)
        for d in range(1, his):
            h = turned(d)
            out_b[o, h] = with_mate(h, parts[d - 1]).astype(jnp.bfloat16)
            sum_hi(o, d).start()
        gate_mate(o).wait_recv()
        gate = split_gate(join_gate(gate_out_a[o]) + join_gate(gate_in_a[o]))
        gate_out_b[o] = gate
        gate_in_b[o, hi] = gate
        for d in range(1, his):
            gate_hi(o, d).start()
        mine[o] = with_mate(hi, back(me))

    def add_hi(o):
        total = mine[o]
        for d in range(1, his):
            sum_from_hi(o, d).wait_recv()
            total = total + in_b[o, turned(d)].astype(jnp.float32)
        out_h[o] = total.astype(jnp.bfloat16)

        @pl.when(o > 0)
        def _():
            to_home(o).start()

        for d in range(1, his):
            gate_from_hi(o, d).wait_recv()
        gate = join_gate(gate_in_b[o, 0])
        for h in range(1, his):
            gate = gate + join_gate(gate_in_b[o, h])
        gate_out_h[o] = split_gate(gate)

        @pl.when(o > 0)
        def _():
            gate_home(o).start()

    def step(i, carry):
        @pl.when(i + 1 < GROUP)
        def _():
            spread(i + 1)

        compute(i)
        return carry

    lax.fori_loop(0, GROUP, step, 0)
    add_hi(GROUP - 1)

    gates = [stand_up(fixed_ref[k:k + 1, :].astype(jnp.float32)) / 65536.0 for k in range(2)]
    total = jnp.zeros((tokens, feat), jnp.float32)
    gate_total = [jnp.zeros((tokens, LANES), jnp.float32) for _ in range(2)]
    for o in range(GROUP):
        if o > 0:
            to_home(o).wait_recv()
        home = out_h if o == 0 else in_h
        hits = [routes[k] == float(o) for k in range(2)]
        weight = sum(jnp.where(hits[k], gates[k], 0.0) for k in range(2))[:, 0:1]
        total = total + weight * dot(table[o], home[o])
    for o in range(GROUP):
        if o > 0:
            gate_home(o).wait_recv()
        home = gate_out_h if o == 0 else gate_in_h
        pair = dot(table[o], home[o][:, 0:CAPACITY], NT)
        value = pair[:, 0:1] + pair[:, 8:9]
        for k in range(2):
            gate_total[k] = gate_total[k] + jnp.where(routes[k] == float(o), value, 0.0)
    out_ref[...] = total.astype(jnp.bfloat16)
    for k in range(2):
        ggrad_ref[k:k + 1, :] = gate_total[k].T[0:1]

    def finish(o, carry):
        for k in range(2):
            for d in range(1, his):
                to_hi(o, k, d).wait_send()
            for h in range(his):
                to_mate(o, k, h).wait_send()
        gate_mate(o).wait_send()
        for h in range(his):
            sum_mate(o, h).wait_send()
        for d in range(1, his):
            sum_hi(o, d).wait_send()
            gate_hi(o, d).wait_send()

        @pl.when(o > 0)
        def _():
            for k in range(2):
                to_node(o, k).wait_send()
            to_home(o).wait_send()
            gate_home(o).wait_send()

        return carry

    lax.fori_loop(0, GROUP, finish, 0)


def body(nodes, locals_, layer_input, output_grad, gate_weight, up_weight, down_weight, route, fixed):
    tokens, feat = layer_input.shape
    width, hidden = gate_weight.shape[1:]
    his = locals_ // 2
    bf16, f32, i32 = jnp.bfloat16, jnp.float32, jnp.int32
    vmem, dma = pltpu.VMEM, pltpu.SemaphoreType.DMA
    routed = GROUP * CAPACITY
    scratch = [
        vmem((tokens, feat), bf16),
        vmem((tokens, feat), bf16),
        vmem((width, hidden), bf16),
        vmem((width, hidden), bf16),
        vmem((hidden, width), bf16),
        vmem((2, tokens), i32),
        vmem((2, tokens), i32),
        vmem((GROUP, tokens, CAPACITY), bf16),
        vmem((GROUP, 2, CAPACITY, feat), bf16),
        vmem((GROUP, locals_, 2, CAPACITY, feat), bf16),
        vmem((GROUP, his, CAPACITY, feat), bf16),
        vmem((GROUP, his, CAPACITY, feat), bf16),
        vmem((GROUP, his, CAPACITY, feat), bf16),
        vmem((GROUP, his, CAPACITY, feat), bf16),
        vmem((GROUP, CAPACITY, feat), f32),
        vmem((GROUP, CAPACITY, feat), bf16),
        vmem((GROUP, CAPACITY, feat), bf16),
        vmem((GROUP, 16, LANES), bf16),
        vmem((GROUP, 16, LANES), bf16),
        vmem((GROUP, 16, LANES), bf16),
        vmem((GROUP, his, 16, LANES), bf16),
        vmem((GROUP, 16, LANES), bf16),
        vmem((GROUP, 16, LANES), bf16),
        dma((7,)),
        dma((GROUP, 2)),
        dma((GROUP, 2)),
        dma((GROUP, 2, his)),
        dma((GROUP, 2, his)),
        dma((GROUP, 2, his)),
        dma((GROUP, 2, his)),
        dma((GROUP, his)),
        dma((GROUP, his)),
        dma((GROUP, his)),
        dma((GROUP, his)),
        dma((GROUP,)),
        dma((GROUP,)),
        dma((GROUP,)),
        dma((GROUP,)),
        dma((GROUP, his)),
        dma((GROUP, his)),
        dma((GROUP,)),
        dma((GROUP,)),
    ]
    in_vmem, anywhere = pl.BlockSpec(memory_space=pltpu.VMEM), pl.BlockSpec(memory_space=pl.ANY)
    grads, gate_grads = pl.pallas_call(
        functools.partial(kernel, nodes, locals_),
        out_shape=(
            jax.ShapeDtypeStruct((tokens, feat), bf16),
            jax.ShapeDtypeStruct((2, tokens), f32),
        ),
        in_specs=[anywhere] * 7,
        out_specs=(in_vmem, in_vmem),
        scratch_shapes=scratch,
        compiler_params=pltpu.CompilerParams(
            collective_id=0, has_side_effects=True, vmem_limit_bytes=60 * 1024 * 1024
        ),
        cost_estimate=pl.CostEstimate(
            flops=10 * routed * width * hidden,
            bytes_accessed=6 * width * hidden + 6 * tokens * feat,
            transcendentals=routed * hidden,
        ),
    )(layer_input, output_grad, gate_weight, up_weight, down_weight, route.T, fixed.T)
    return grads, gate_grads.T


def solution(mesh):
    in_specs = (
        P("node", "local"),
        P("node", "local"),
        P("node", None, "local"),
        P("node", None, "local"),
        P("node", "local", None),
        P("node", None),
        P("node", None),
    )
    out_specs = (P("node", "local"), P("node", None))
    run = functools.partial(body, mesh.shape["node"], mesh.shape["local"])
    return jax.shard_map(run, mesh=mesh, in_specs=in_specs, out_specs=out_specs, check_vma=False)
```

time: 66.8 us -> 65.2 us (0.976)
  the two profiles are of different devices: /device:TPU:26 before, /device:TPU:3 now
where the time goes in v2:
time: 65.2 us; the launch traced here: 65 us
  Pallas kernels  61.5 us (94%)
  local copies, waits for them, and re-layouts  2.84 us (4%)
    pallas_call x1, Pallas kernels, body(): pl.pallas_call(functools.partial(kernel, nodes, locals_), out_shape=(jax....  61.5 us
    unnamed x2, local copies, waits for them, and re-layouts  2.84 us

profile of v2, /device:TPU:3, one launch (start us, length us, event | category | flops | bytes accessed | tf_op | source)
XLA Modules:
  0.0 65.0 jit_solution(7613044667368002275)
XLA Ops:
  0.6 61.5 %shard_map.86 = (bf16[128,896]{1,0:T(8,128)(2,1)}, f32[2,128]{1,0:T(2,128)}) custom-call(bf16[128,896]{1,0:T(8,128)(2,1)} %x_hbm.1, bf16[128,896]{1,0:T(8,128)(2,1)} %g_hbm.1, bf16[1,3584,256]{2,1,0:T(8,128)(2,1)} %gate_hbm.1, bf16[1,3584,256]{2,1,0:T(8,128)(2,1)} %up_hbm.1, bf16[1,256,3584]{2,1,0:T(8,128)(2,1)} %down_hbm.1, s32[2,128]{1,0:T(2,128)} %bitcast.4, ...), custom_call_target="tpu_custom_call" | custom-call | flops 2936012800 | bytes 6193152 | tf_op jit(solution)/shard_map/pallas_call | solution.py:397
  62.2 1.6 %copy.11 = bf16[128,896]{1,0:T(8,128)(2,1)} copy(bf16[128,896]{1,0:T(8,128)(2,1)} %get-tuple-element.8) | data formatting | bytes 458752
  63.8 1.2 %copy.12 = f32[128,2]{0,1:T(2,128)} copy(f32[128,2]{0,1:T(2,128)} %bitcast.3) | data formatting | bytes 2048

commit v3 on v2

--- a/solution.py
+++ b/solution.py
@@ -9,6 +9,7 @@
 
 GROUP = 4
 CAPACITY = 80
+ORDER = (0, 2, 3, 1)
 LANES = 128
 MESH = pl.DeviceIdType.MESH
 NT = (((1,), (1,)), ((), ()))
@@ -62,6 +63,9 @@
     def beside(index):
         return (node, index)
 
+    def offset(p):
+        return (p % 3 + 1) * ((p + 3) // 4)
+
     def turned(d):
         return lax.rem(hi + d, his)
 
@@ -89,7 +93,7 @@
         )
 
     def to_node(o, k):
-        return remote(packed.at[o, k], got.at[o, me, k], ns.at[o, k], nr.at[o, k], ahead(o))
+        return remote(packed.at[o, k], got.at[o, me, k], ns.at[o, k], nr.at[o, k], ahead(offset(o)))
 
     def to_hi(o, k, d):
         return remote(
@@ -122,7 +126,7 @@
         return remote(out_b.at[o, h], in_b.at[o, h], sb.at[o, h], rb.at[o, h], beside(h * 2 + lo))
 
     def to_home(o):
-        return remote(out_h.at[o], in_h.at[o], sm.at[o], rm.at[o], ahead(-o))
+        return remote(out_h.at[o], in_h.at[o], sm.at[o], rm.at[o], ahead(-offset(o)))
 
     def gate_mate(o):
         return remote(gate_out_a.at[o], gate_in_a.at[o], sga.at[o], rga.at[o], beside(mate))
@@ -140,7 +144,7 @@
         )
 
     def gate_home(o):
-        return remote(gate_out_h.at[o], gate_in_h.at[o], sgm.at[o], rgm.at[o], ahead(-o))
+        return remote(gate_out_h.at[o], gate_in_h.at[o], sgm.at[o], rgm.at[o], ahead(-offset(o)))
 
     fetches[0].wait()
     lanes = lax.broadcasted_iota(jnp.int32, (tokens, LANES), 1).astype(jnp.float32)
@@ -153,7 +157,8 @@
     slots = lax.broadcasted_iota(jnp.int32, (tokens, CAPACITY), 1).astype(jnp.float32) + 1.0
     tables = []
     for o in range(GROUP):
-        here = (ranks[:, o:o + 1] == slots) & (chosen[:, o:o + 1] > 0.5)
+        at = slice(ORDER[o], ORDER[o] + 1)
+        here = (ranks[:, at] == slots) & (chosen[:, at] > 0.5)
         tables.append(here.astype(jnp.float32).astype(jnp.bfloat16))
         table[o] = tables[o]
 
@@ -174,17 +179,22 @@
         to_hi(0, 1, d).start()
     packed[1, 1] = pack(1, 1)
     to_node(1, 1).start()
+    for k in range(2):
+        to_mate(0, k, hi).start()
     for o in range(2, GROUP):
         for k in range(2):
             packed[o, k] = pack(o, k)
-            to_node(o, k).start()
-    for k in range(2):
-        to_mate(0, k, hi).start()
     for copy in fetches[3:]:
         copy.wait()
 
     def spread(o):
         for k in range(2):
+            to_node(o, k).wait_send()
+
+            @pl.when(o + 1 < GROUP)
+            def _():
+                to_node(o + 1, k).start()
+
             to_node(o, k).wait_recv()
             for d in range(1, his):
                 to_hi(o, k, d).start()
@@ -302,7 +312,7 @@
         if o > 0:
             to_home(o).wait_recv()
         home = out_h if o == 0 else in_h
-        hits = [routes[k] == float(o) for k in range(2)]
+        hits = [routes[k] == float(ORDER[o]) for k in range(2)]
         weight = sum(jnp.where(hits[k], gates[k], 0.0) for k in range(2))[:, 0:1]
         total = total + weight * dot(table[o], home[o])
     for o in range(GROUP):
@@ -312,7 +322,7 @@
         pair = dot(table[o], home[o][:, 0:CAPACITY], NT)
         value = pair[:, 0:1] + pair[:, 8:9]
         for k in range(2):
-            gate_total[k] = gate_total[k] + jnp.where(routes[k] == float(o), value, 0.0)
+            gate_total[k] = gate_total[k] + jnp.where(routes[k] == float(ORDER[o]), value, 0.0)
     out_ref[...] = total.astype(jnp.bfloat16)
     for k in range(2):
         ggrad_ref[k:k + 1, :] = gate_total[k].T[0:1]
@@ -332,8 +342,6 @@
 
         @pl.when(o > 0)
         def _():
-            for k in range(2):
-                to_node(o, k).wait_send()
             to_home(o).wait_send()
             gate_home(o).wait_send()
 
@@ -404,7 +412,7 @@
         out_specs=(in_vmem, in_vmem),
         scratch_shapes=scratch,
         compiler_params=pltpu.CompilerParams(
-            collective_id=0, has_side_effects=True, vmem_limit_bytes=60 * 1024 * 1024
+            collective_id=0, has_side_effects=True, vmem_limit_bytes=48 * 1024 * 1024
         ),
         cost_estimate=pl.CostEstimate(
             flops=10 * routed * width * hidden,

time: 65.2 us -> 76.2 us (1.17)
  the two profiles are of different devices: /device:TPU:3 before, /device:TPU:26 now
where the time goes in v3:
time: 76.2 us; the launch traced here: 75.9 us
  Pallas kernels  66.2 us (87%)
  local copies, waits for them, and re-layouts  8.98 us (12%)
    pallas_call x1, Pallas kernels, body(): pl.pallas_call(functools.partial(kernel, nodes, locals_), out_shape=(jax....  66.2 us
    unnamed x16, local copies, waits for them, and re-layouts  8.98 us

profile of v3, /device:TPU:26, one launch (start us, length us, event | category | flops | bytes accessed | tf_op | source)
XLA Modules:
  0.0 75.9 jit_solution(4716872419764652252)
XLA Ops:
  0.6 0.0 copy-start
  0.6 1.5 %copy-done = bf16[1,3584,256]{2,1,0:T(8,128)(2,1)S(1)} copy-done((bf16[1,3584,256]{2,1,0:T(8,128)(2,1)S(1)}, bf16[1,3584,256]{2,1,0:T(8,128)(2,1)}, u32[]{:S(2)}) %copy-start) | copy-done | bytes 1835032
  2.1 0.0 copy-start.1
  2.1 1.5 %copy-done.1 = bf16[1,3584,256]{2,1,0:T(8,128)(2,1)S(1)} copy-done((bf16[1,3584,256]{2,1,0:T(8,128)(2,1)S(1)}, bf16[1,3584,256]{2,1,0:T(8,128)(2,1)}, u32[]{:S(2)}) %copy-start.1) | copy-done | bytes 1835032
  3.6 0.0 copy-start.2
  3.6 1.5 %copy-done.2 = bf16[1,256,3584]{2,1,0:T(8,128)(2,1)S(1)} copy-done((bf16[1,256,3584]{2,1,0:T(8,128)(2,1)S(1)}, bf16[1,256,3584]{2,1,0:T(8,128)(2,1)}, u32[]{:S(2)}) %copy-start.2) | copy-done | bytes 1835032
  5.1 0.0 copy-start.3
  5.1 0.9 %copy-done.3 = bf16[128,896]{1,0:T(8,128)(2,1)S(1)} copy-done((bf16[128,896]{1,0:T(8,128)(2,1)S(1)}, bf16[128,896]{1,0:T(8,128)(2,1)}, u32[]{:S(2)}) %copy-start.3) | copy-done | bytes 229400
  6.1 0.0 copy-start.4
  6.1 0.9 %copy-done.4 = bf16[128,896]{1,0:T(8,128)(2,1)S(1)} copy-done((bf16[128,896]{1,0:T(8,128)(2,1)S(1)}, bf16[128,896]{1,0:T(8,128)(2,1)}, u32[]{:S(2)}) %copy-start.4) | copy-done | bytes 229400
  7.0 0.0 copy-start.5
  7.0 0.7 copy-done.5
  7.7 0.0 copy-start.6
  7.7 0.7 copy-done.6
  8.4 66.2 %shard_map.86 = (bf16[128,896]{1,0:T(8,128)(2,1)S(1)}, f32[2,128]{1,0:T(2,128)S(1)}) custom-call(bf16[128,896]{1,0:T(8,128)(2,1)S(1)} %copy-done.3, bf16[128,896]{1,0:T(8,128)(2,1)S(1)} %copy-done.4, bf16[1,3584,256]{2,1,0:T(8,128)(2,1)S(1)} %copy-done, bf16[1,3584,256]{2,1,0:T(8,128)(2,1)S(1)} %copy-done.1, bf16[1,256,3584]{2,1,0:T(8,128)(2,1)S(1)} %copy-done.2, ...), custom_call_target="tpu_custom_call" | custom-call | flops 2936012800 | bytes 6193152 | tf_op jit(solution)/shard_map/pallas_call | solution.py:405
  74.6 0.7 copy.11
  75.3 0.6 copy.12
Async XLA Ops:
  0.6 1.5 %copy-start = (bf16[1,3584,256]{2,1,0:T(8,128)(2,1)S(1)}, bf16[1,3584,256]{2,1,0:T(8,128)(2,1)}, u32[]{:S(2)}) copy-start(bf16[1,3584,256]{2,1,0:T(8,128)(2,1)} %gate_hbm.1) | copy-start | bytes 5505028
  2.1 1.5 %copy-start.1 = (bf16[1,3584,256]{2,1,0:T(8,128)(2,1)S(1)}, bf16[1,3584,256]{2,1,0:T(8,128)(2,1)}, u32[]{:S(2)}) copy-start(bf16[1,3584,256]{2,1,0:T(8,128)(2,1)} %up_hbm.1) | copy-start | bytes 5505028
  3.6 1.5 %copy-start.2 = (bf16[1,256,3584]{2,1,0:T(8,128)(2,1)S(1)}, bf16[1,256,3584]{2,1,0:T(8,128)(2,1)}, u32[]{:S(2)}) copy-start(bf16[1,256,3584]{2,1,0:T(8,128)(2,1)} %down_hbm.1) | copy-start | bytes 5505028
  5.1 0.9 %copy-start.3 = (bf16[128,896]{1,0:T(8,128)(2,1)S(1)}, bf16[128,896]{1,0:T(8,128)(2,1)}, u32[]{:S(2)}) copy-start(bf16[128,896]{1,0:T(8,128)(2,1)} %x_hbm.1) | copy-start | bytes 688132
  6.1 0.9 %copy-start.4 = (bf16[128,896]{1,0:T(8,128)(2,1)S(1)}, bf16[128,896]{1,0:T(8,128)(2,1)}, u32[]{:S(2)}) copy-start(bf16[128,896]{1,0:T(8,128)(2,1)} %g_hbm.1) | copy-start | bytes 688132
  7.0 0.7 copy-start.5
  7.7 0.7 copy-start.6

commit v4 on v2

--- a/solution.py
+++ b/solution.py
@@ -48,7 +48,8 @@
     x_ref, g_ref, gw, uw, dw, route_ref, fixed_ref,
     table, packed, got, out_a, in_a, out_b, in_b, mine, out_h, in_h,
     gate_out_a, gate_in_a, gate_out_b, gate_in_b, gate_out_h, gate_in_h,
-    wsem, ns, nr, hs, hr, ls, lr, sa, ra, sb, rb, sm, rm, sga, rga, sgb, rgb, sgm, rgm,
+    relay,
+    wsem, es, er, ns, nr, hs, hr, ls, lr, sa, ra, sb, rb, sm, rm, sga, rga, sgb, rgb, sgm, rgm,
 ):
     tokens, feat = x_ref.shape
     his = locals_ // 2
@@ -90,6 +91,26 @@
 
     def to_node(o, k):
         return remote(packed.at[o, k], got.at[o, me, k], ns.at[o, k], nr.at[o, k], ahead(o))
+
+    far = GROUP - 1
+    legs = nodes % 2 == 0
+    odd = lax.rem(node, 2) == 1
+
+    def first_leg(k):
+        return remote(packed.at[far, k], relay.at[k], es.at[k], er.at[k], ahead(1))
+
+    def second_leg(k):
+        return remote(
+            relay.at[k], got.at[far, me, k], es.at[k], nr.at[far, k], ahead(far - 1)
+        )
+
+    def pass_legs():
+        if legs:
+            @pl.when(jnp.logical_not(odd))
+            def _():
+                for k in range(2):
+                    first_leg(k).wait_recv()
+                    second_leg(k).start()
 
     def to_hi(o, k, d):
         return remote(
@@ -163,21 +184,37 @@
 
     fetches[1].wait()
     got[0, me, 0] = pack(0, 0)
+    packed[far, 0] = pack(far, 0)
     packed[1, 0] = pack(1, 0)
     fetches[2].wait()
     pl.semaphore_wait(barrier, len(friends))
-    for d in range(1, his):
-        to_hi(0, 0, d).start()
-    to_node(1, 0).start()
+
+    def first_sends(k):
+        for d in range(1, his):
+            to_hi(0, k, d).start()
+        if legs:
+            @pl.when(odd)
+            def _():
+                first_leg(k).start()
+
+        to_node(1, k).start()
+
+    first_sends(0)
     got[0, me, 1] = pack(0, 1)
-    for d in range(1, his):
-        to_hi(0, 1, d).start()
+    packed[far, 1] = pack(far, 1)
     packed[1, 1] = pack(1, 1)
-    to_node(1, 1).start()
-    for o in range(2, GROUP):
+    first_sends(1)
+    for o in range(2, far):
         for k in range(2):
             packed[o, k] = pack(o, k)
             to_node(o, k).start()
+    for k in range(2):
+        if legs:
+            @pl.when(jnp.logical_not(odd))
+            def _():
+                to_node(far, k).start()
+        else:
+            to_node(far, k).start()
     for k in range(2):
         to_mate(0, k, hi).start()
     for copy in fetches[3:]:
@@ -288,6 +325,10 @@
         @pl.when(i + 1 < GROUP)
         def _():
             spread(i + 1)
+
+        @pl.when(i == 0)
+        def _():
+            pass_legs()
 
         compute(i)
         return carry
@@ -330,16 +371,31 @@
             sum_hi(o, d).wait_send()
             gate_hi(o, d).wait_send()
 
-        @pl.when(o > 0)
+        @pl.when((o > 0) & (o < far))
         def _():
             for k in range(2):
                 to_node(o, k).wait_send()
+
+        @pl.when(o > 0)
+        def _():
             to_home(o).wait_send()
             gate_home(o).wait_send()
 
         return carry
 
     lax.fori_loop(0, GROUP, finish, 0)
+    for k in range(2):
+        if legs:
+            @pl.when(odd)
+            def _():
+                first_leg(k).wait_send()
+
+            @pl.when(jnp.logical_not(odd))
+            def _():
+                second_leg(k).wait_send()
+                to_node(far, k).wait_send()
+        else:
+            to_node(far, k).wait_send()
 
 
 def body(nodes, locals_, layer_input, output_grad, gate_weight, up_weight, down_weight, route, fixed):
@@ -373,7 +429,10 @@
         vmem((GROUP, his, 16, LANES), bf16),
         vmem((GROUP, 16, LANES), bf16),
         vmem((GROUP, 16, LANES), bf16),
+        vmem((2, CAPACITY, feat), bf16),
         dma((7,)),
+        dma((2,)),
+        dma((2,)),
         dma((GROUP, 2)),
         dma((GROUP, 2)),
         dma((GROUP, 2, his)),
@@ -393,18 +452,18 @@
         dma((GROUP,)),
         dma((GROUP,)),
     ]
-    in_vmem, anywhere = pl.BlockSpec(memory_space=pltpu.VMEM), pl.BlockSpec(memory_space=pl.ANY)
+    in_vmem, in_hbm = pl.BlockSpec(memory_space=pltpu.VMEM), pl.BlockSpec(memory_space=pltpu.HBM)
     grads, gate_grads = pl.pallas_call(
         functools.partial(kernel, nodes, locals_),
         out_shape=(
             jax.ShapeDtypeStruct((tokens, feat), bf16),
             jax.ShapeDtypeStruct((2, tokens), f32),
         ),
-        in_specs=[anywhere] * 7,
+        in_specs=[in_hbm] * 7,
         out_specs=(in_vmem, in_vmem),
         scratch_shapes=scratch,
         compiler_params=pltpu.CompilerParams(
-            collective_id=0, has_side_effects=True, vmem_limit_bytes=60 * 1024 * 1024
+            collective_id=0, has_side_effects=True, vmem_limit_bytes=48 * 1024 * 1024
         ),
         cost_estimate=pl.CostEstimate(
             flops=10 * routed * width * hidden,

time: 65.2 us -> 77.9 us (1.19)
  Pallas kernels: 61.5 us -> 67.9 us
  local copies, waits for them, and re-layouts: 2.84 us -> 8.98 us
    pallas_call x1, Pallas kernels: 61.5 us -> 67.9 us  [body(): pl.pallas_call(functools.partial(kernel, nodes, locals_), out_shape=(jax....]
    unnamed x2 -> x16, local copies, waits for them, and re-layouts: 2.84 us -> 8.98 us
where the time goes in v4:
time: 77.9 us; the launch traced here: 77.6 us
  Pallas kernels  67.9 us (87%)
  local copies, waits for them, and re-layouts  8.98 us (12%)
    pallas_call x1, Pallas kernels, body(): pl.pallas_call(functools.partial(kernel, nodes, locals_), out_shape=(jax....  67.9 us
    unnamed x16, local copies, waits for them, and re-layouts  8.98 us

profile of v4, /device:TPU:3, one launch (start us, length us, event | category | flops | bytes accessed | tf_op | source)
XLA Modules:
  0.0 77.6 jit_solution(8557488545244350110)
XLA Ops:
  0.6 0.0 copy-start
  0.6 1.5 %copy-done = bf16[1,3584,256]{2,1,0:T(8,128)(2,1)S(1)} copy-done((bf16[1,3584,256]{2,1,0:T(8,128)(2,1)S(1)}, bf16[1,3584,256]{2,1,0:T(8,128)(2,1)}, u32[]{:S(2)}) %copy-start) | copy-done | bytes 1835032
  2.1 0.0 copy-start.1
  2.1 1.5 %copy-done.1 = bf16[1,3584,256]{2,1,0:T(8,128)(2,1)S(1)} copy-done((bf16[1,3584,256]{2,1,0:T(8,128)(2,1)S(1)}, bf16[1,3584,256]{2,1,0:T(8,128)(2,1)}, u32[]{:S(2)}) %copy-start.1) | copy-done | bytes 1835032
  3.6 0.0 copy-start.2
  3.6 1.5 %copy-done.2 = bf16[1,256,3584]{2,1,0:T(8,128)(2,1)S(1)} copy-done((bf16[1,256,3584]{2,1,0:T(8,128)(2,1)S(1)}, bf16[1,256,3584]{2,1,0:T(8,128)(2,1)}, u32[]{:S(2)}) %copy-start.2) | copy-done | bytes 1835032
  5.1 0.0 copy-start.3
  5.1 0.9 %copy-done.3 = bf16[128,896]{1,0:T(8,128)(2,1)S(1)} copy-done((bf16[128,896]{1,0:T(8,128)(2,1)S(1)}, bf16[128,896]{1,0:T(8,128)(2,1)}, u32[]{:S(2)}) %copy-start.3) | copy-done | bytes 229400
  6.1 0.0 copy-start.4
  6.1 0.9 %copy-done.4 = bf16[128,896]{1,0:T(8,128)(2,1)S(1)} copy-done((bf16[128,896]{1,0:T(8,128)(2,1)S(1)}, bf16[128,896]{1,0:T(8,128)(2,1)}, u32[]{:S(2)}) %copy-start.4) | copy-done | bytes 229400
  7.0 0.0 copy-start.5
  7.0 0.7 copy-done.5
  7.7 0.0 copy-start.6
  7.7 0.7 copy-done.6
  8.4 67.9 %shard_map.86 = (bf16[128,896]{1,0:T(8,128)(2,1)S(1)}, f32[2,128]{1,0:T(2,128)S(1)}) custom-call(bf16[128,896]{1,0:T(8,128)(2,1)S(1)} %copy-done.3, bf16[128,896]{1,0:T(8,128)(2,1)S(1)} %copy-done.4, bf16[1,3584,256]{2,1,0:T(8,128)(2,1)S(1)} %copy-done, bf16[1,3584,256]{2,1,0:T(8,128)(2,1)S(1)} %copy-done.1, bf16[1,256,3584]{2,1,0:T(8,128)(2,1)S(1)} %copy-done.2, ...), custom_call_target="tpu_custom_call" | custom-call | flops 2936012800 | bytes 6193152 | tf_op jit(solution)/shard_map/pallas_call | solution.py:456
  76.3 0.7 copy.11
  77.0 0.6 copy.12
Async XLA Ops:
  0.6 1.5 %copy-start = (bf16[1,3584,256]{2,1,0:T(8,128)(2,1)S(1)}, bf16[1,3584,256]{2,1,0:T(8,128)(2,1)}, u32[]{:S(2)}) copy-start(bf16[1,3584,256]{2,1,0:T(8,128)(2,1)} %gate_hbm.1) | copy-start | bytes 5505028
  2.1 1.5 %copy-start.1 = (bf16[1,3584,256]{2,1,0:T(8,128)(2,1)S(1)}, bf16[1,3584,256]{2,1,0:T(8,128)(2,1)}, u32[]{:S(2)}) copy-start(bf16[1,3584,256]{2,1,0:T(8,128)(2,1)} %up_hbm.1) | copy-start | bytes 5505028
  3.6 1.5 %copy-start.2 = (bf16[1,256,3584]{2,1,0:T(8,128)(2,1)S(1)}, bf16[1,256,3584]{2,1,0:T(8,128)(2,1)}, u32[]{:S(2)}) copy-start(bf16[1,256,3584]{2,1,0:T(8,128)(2,1)} %down_hbm.1) | copy-start | bytes 5505028
  5.1 0.9 %copy-start.3 = (bf16[128,896]{1,0:T(8,128)(2,1)S(1)}, bf16[128,896]{1,0:T(8,128)(2,1)}, u32[]{:S(2)}) copy-start(bf16[128,896]{1,0:T(8,128)(2,1)} %x_hbm.1) | copy-start | bytes 688132
  6.1 0.9 %copy-start.4 = (bf16[128,896]{1,0:T(8,128)(2,1)S(1)}, bf16[128,896]{1,0:T(8,128)(2,1)}, u32[]{:S(2)}) copy-start(bf16[128,896]{1,0:T(8,128)(2,1)} %g_hbm.1) | copy-start | bytes 688132
  7.0 0.7 copy-start.5
  7.7 0.7 copy-start.6

commit v5 on v2

v5 whole, which is shorter than its diff:
```python
import functools

import jax
import jax.numpy as jnp
from jax import lax
from jax.experimental import pallas as pl
from jax.experimental.pallas import tpu as pltpu
from jax.sharding import PartitionSpec as P

GROUP = 4
CAPACITY = 80
ORDER = (0, 3, 1, 2)
PAIR = 2
BATCHES = GROUP // PAIR
LANES = 128
MESH = pl.DeviceIdType.MESH
NT = (((1,), (1,)), ((), ()))
TN = (((0,), (0,)), ((), ()))


def dot(a, b, dims=None):
    if dims is None:
        return jnp.dot(a, b, preferred_element_type=jnp.float32)
    return lax.dot_general(a, b, dims, preferred_element_type=jnp.float32)


def split_gate(value):
    high = value.astype(jnp.bfloat16).astype(jnp.float32)
    return jnp.concatenate((high, value - high), axis=0).astype(jnp.bfloat16)


def join_gate(parts):
    parts = parts.astype(jnp.float32)
    return parts[0:8] + parts[8:16]


def lay_down(column):
    wide = jnp.broadcast_to(column, (CAPACITY, LANES))
    rest = jnp.zeros((LANES - CAPACITY, LANES), jnp.float32)
    return jnp.concatenate((wide, rest), axis=0).T[0:8]


def stand_up(row):
    return jnp.broadcast_to(row, (LANES, row.shape[1])).T


def kernel(
    nodes, locals_,
    x_hbm, g_hbm, gate_hbm, up_hbm, down_hbm, route_hbm, fixed_hbm,
    out_ref, ggrad_ref,
    x_ref, g_ref, gu, dw, route_ref, fixed_ref,
    table, packed, got, out_a, in_a, out_b, in_b, mine, out_h, in_h,
    gate_out_a, gate_in_a, gate_out_b, gate_in_b, gate_out_h, gate_in_h,
    wsem, ns, nr, hs, hr, ls, lr, sa, ra, sb, rb, sm, rm, sga, rga, sgb, rgb, sgm, rgm,
):
    tokens, feat = x_ref.shape
    hidden = dw.shape[0]
    his = locals_ // 2
    node, me = lax.axis_index("node"), lax.axis_index("local")
    hi, lo = me // 2, me % 2
    mate = hi * 2 + (1 - lo)

    def ahead(steps):
        return (lax.rem(node + steps + nodes, nodes), me)

    def beside(index):
        return (node, index)

    def turned(d):
        return lax.rem(hi + d, his)

    fetches = [
        pltpu.make_async_copy(source, dest, wsem.at[i])
        for i, (source, dest) in enumerate((
            (route_hbm, route_ref), (x_hbm, x_ref), (g_hbm, g_ref), (fixed_hbm, fixed_ref),
            (gate_hbm.at[0], gu.at[:, pl.ds(0, hidden)]),
            (up_hbm.at[0], gu.at[:, pl.ds(hidden, hidden)]),
            (down_hbm.at[0], dw),
        ))
    ]
    for copy in fetches:
        copy.start()

    barrier = pltpu.get_barrier_semaphore()
    friends = [ahead(s) for o in range(1, GROUP) for s in (o, -o)]
    friends += [beside(turned(d) * 2 + lo) for d in range(1, his)]
    friends += [beside(mate)]
    for friend in friends:
        pl.semaphore_signal(barrier, inc=1, device_id=friend, device_id_type=MESH)

    def remote(source, dest, send, recv, device):
        return pltpu.make_async_remote_copy(
            src_ref=source, dst_ref=dest, send_sem=send, recv_sem=recv,
            device_id=device, device_id_type=MESH,
        )

    def slot(o, l, k):
        return got.at[o // PAIR, l, k, pl.ds(o % PAIR * CAPACITY, CAPACITY)]

    def block_of(buffer, o, rows):
        return buffer.at[o // PAIR, pl.ds(o % PAIR * rows, rows)]

    def to_node(o, k):
        return remote(packed.at[o, k], slot(o, me, k), ns.at[o, k], nr.at[o, k], ahead(ORDER[o]))

    def to_hi(o, k, d):
        mine_ = slot(o, me, k)
        return remote(mine_, mine_, hs.at[o, k, d], hr.at[o, k, hi], beside(turned(d) * 2 + lo))

    def from_hi(o, k, d):
        h = turned(d)
        its = slot(o, h * 2 + lo, k)
        return remote(its, its, hs.at[o, k, d], hr.at[o, k, h], beside(h * 2 + lo))

    def to_mate(o, k, h):
        its = slot(o, h * 2 + lo, k)
        return remote(its, its, ls.at[o, k, h], lr.at[o, k, h], beside(mate))

    def from_mate(o, k, h):
        its = slot(o, h * 2 + 1 - lo, k)
        return remote(its, its, ls.at[o, k, h], lr.at[o, k, h], beside(mate))

    def sum_mate(b, h):
        return remote(out_a.at[b, h], in_a.at[b, h], sa.at[b, h], ra.at[b, h], beside(mate))

    def sum_hi(b, d):
        h = turned(d)
        return remote(out_b.at[b, h], in_b.at[b, hi], sb.at[b, h], rb.at[b, hi], beside(h * 2 + lo))

    def sum_from_hi(b, d):
        h = turned(d)
        return remote(out_b.at[b, h], in_b.at[b, h], sb.at[b, h], rb.at[b, h], beside(h * 2 + lo))

    def to_home(o):
        return remote(
            block_of(out_h, o, CAPACITY), block_of(in_h, o, CAPACITY),
            sm.at[o], rm.at[o], ahead(-ORDER[o]),
        )

    def gate_mate(b):
        return remote(gate_out_a.at[b], gate_in_a.at[b], sga.at[b], rga.at[b], beside(mate))

    def gate_hi(b, d):
        h = turned(d)
        return remote(
            gate_out_b.at[b], gate_in_b.at[b, hi], sgb.at[b, h], rgb.at[b, hi], beside(h * 2 + lo)
        )

    def gate_from_hi(b, d):
        h = turned(d)
        return remote(
            gate_out_b.at[b], gate_in_b.at[b, h], sgb.at[b, h], rgb.at[b, h], beside(h * 2 + lo)
        )

    def gate_home(o):
        return remote(
            block_of(gate_out_h, o, 16), block_of(gate_in_h, o, 16),
            sgm.at[o], rgm.at[o], ahead(-ORDER[o]),
        )

    fetches[0].wait()
    lanes = lax.broadcasted_iota(jnp.int32, (tokens, LANES), 1).astype(jnp.float32)
    routes = [stand_up(route_ref[k:k + 1, :].astype(jnp.float32)) for k in range(2)]
    chosen = ((routes[0] == lanes) | (routes[1] == lanes)).astype(jnp.float32)
    row = lax.broadcasted_iota(jnp.int32, (tokens, tokens), 0)
    column = lax.broadcasted_iota(jnp.int32, (tokens, tokens), 1)
    below = (column <= row).astype(jnp.float32).astype(jnp.bfloat16)
    ranks = dot(below, chosen.astype(jnp.bfloat16))
    slots = lax.broadcasted_iota(jnp.int32, (tokens, CAPACITY), 1).astype(jnp.float32) + 1.0
    tables = []
    for o in range(GROUP):
        at = slice(ORDER[o], ORDER[o] + 1)
        here = (ranks[:, at] == slots) & (chosen[:, at] > 0.5)
        tables.append(here.astype(jnp.float32).astype(jnp.bfloat16))
        table[o] = tables[o]

    def pack(o, k):
        source = x_ref if k == 0 else g_ref
        return dot(tables[o], source[...], TN).astype(jnp.bfloat16)

    fetches[1].wait()
    got[0, me, 0, pl.ds(0, CAPACITY)] = pack(0, 0)
    packed[1, 0] = pack(1, 0)
    fetches[2].wait()
    pl.semaphore_wait(barrier, len(friends))
    for d in range(1, his):
        to_hi(0, 0, d).start()
    to_node(1, 0).start()
    got[0, me, 1, pl.ds(0, CAPACITY)] = pack(0, 1)
    for d in range(1, his):
        to_hi(0, 1, d).start()
    packed[1, 1] = pack(1, 1)
    to_node(1, 1).start()
    for o in range(2, GROUP):
        for k in range(2):
            packed[o, k] = pack(o, k)
            to_node(o, k).start()
    for k in range(2):
        to_mate(0, k, hi).start()
    for copy in fetches[3:]:
        copy.wait()

    def spread(o):
        for k in range(2):
            to_node(o, k).wait_recv()
            for d in range(1, his):
                to_hi(o, k, d).start()
            to_mate(o, k, hi).start()

    def pass_on(o, k):
        for d in range(1, his):
            from_hi(o, k, d).wait_recv()
            to_mate(o, k, turned(d)).start()

    def gathered(o, k):
        for h in range(his):
            from_mate(o, k, h).wait_recv()

    def block(l):
        return pl.ds(pl.multiple_of(l * feat, 64), feat)

    def split_rows(rows):
        return jnp.concatenate([split_gate(part) for part in rows], axis=0)

    def join_rows(parts):
        return [join_gate(parts[16 * r:16 * r + 16]) for r in range(PAIR)]

    def pre(b):
        total = None
        for l in range(locals_):
            part = dot(got[b, l, 0], gu[pl.ds(l * feat, feat), :])
            total = part if total is None else total + part
        return total[:, 0:hidden], total[:, hidden:2 * hidden]

    def hidden_grad(b):
        total = None
        for l in range(locals_):
            part = dot(got[b, l, 1], dw[:, pl.ds(l * feat, feat)], NT)
            total = part if total is None else total + part
        return total

    def rest(b, pair, v):
        a, up = pair
        s = 1.0 / (1.0 + jnp.exp(-a))
        swish = a * s
        u = (v * swish).astype(jnp.bfloat16)
        w = (v * up * s * (1.0 + a * (1.0 - s))).astype(jnp.bfloat16)
        both = jnp.concatenate((w, u), axis=1)
        part = jnp.sum(swish * up * v, axis=1, keepdims=True)

        def back(l):
            return dot(both, gu[block(l), :], NT)

        def send_mate(h):
            out_a[b, h] = back(h * 2 + 1 - lo).astype(jnp.bfloat16)
            sum_mate(b, h).start()

        def with_mate(h, own):
            sum_mate(b, h).wait_recv()
            return own + in_a[b, h].astype(jnp.float32)

        for d in range(1, his):
            send_mate(turned(d))
        gate_out_a[b] = split_rows(
            [lay_down(part[CAPACITY * r:CAPACITY * (r + 1)]) for r in range(PAIR)]
        )
        gate_mate(b).start()
        parts = [back(turned(d) * 2 + lo) for d in range(1, his)]
        for d in range(1, his):
            h = turned(d)
            out_b[b, h] = with_mate(h, parts[d - 1]).astype(jnp.bfloat16)
            sum_hi(b, d).start()
        send_mate(hi)
        gate_mate(b).wait_recv()
        gate = split_rows([
            x + y for x, y in zip(join_rows(gate_out_a[b]), join_rows(gate_in_a[b]))
        ])
        gate_out_b[b] = gate
        gate_in_b[b, hi] = gate
        for d in range(1, his):
            gate_hi(b, d).start()
        mine[b] = with_mate(hi, back(me))

    def add_hi(b):
        total = mine[b]
        for d in range(1, his):
            sum_from_hi(b, d).wait_recv()
            total = total + in_b[b, turned(d)].astype(jnp.float32)
        out_h[b] = total.astype(jnp.bfloat16)
        blocks = [o for o in range(b * PAIR, (b + 1) * PAIR) if o > 0]
        for o in blocks:
            to_home(o).start()
        for d in range(1, his):
            gate_from_hi(b, d).wait_recv()
        gate = join_rows(gate_in_b[b, 0])
        for h in range(1, his):
            gate = [x + y for x, y in zip(gate, join_rows(gate_in_b[b, h]))]
        gate_out_h[b] = split_rows(gate)
        for o in blocks:
            gate_home(o).start()

    pass_on(0, 0)
    pass_on(0, 1)
    spread(1)
    pass_on(1, 0)
    for o in (0, 1):
        gathered(o, 0)
    pair = pre(0)
    pass_on(1, 1)
    for o in (0, 1):
        gathered(o, 1)
    v = hidden_grad(0)
    spread(2)
    rest(0, pair, v)
    spread(3)
    pass_on(2, 0)
    pass_on(2, 1)
    pass_on(3, 0)
    for o in (2, 3):
        gathered(o, 0)
    pair = pre(1)
    pass_on(3, 1)
    add_hi(0)
    for o in (2, 3):
        gathered(o, 1)
    v = hidden_grad(1)
    rest(1, pair, v)
    add_hi(1)

    gates = [stand_up(fixed_ref[k:k + 1, :].astype(jnp.float32)) / 65536.0 for k in range(2)]
    total = jnp.zeros((tokens, feat), jnp.float32)
    gate_total = [jnp.zeros((tokens, LANES), jnp.float32) for _ in range(2)]
    for o in range(GROUP):
        if o > 0:
            to_home(o).wait_recv()
        home = block_of(out_h if o == 0 else in_h, o, CAPACITY)
        hits = [routes[k] == float(ORDER[o]) for k in range(2)]
        weight = sum(jnp.where(hits[k], gates[k], 0.0) for k in range(2))[:, 0:1]
        total = total + weight * dot(table[o], home[...])
    for o in range(GROUP):
        if o > 0:
            gate_home(o).wait_recv()
        home = block_of(gate_out_h if o == 0 else gate_in_h, o, 16)
        pair = dot(table[o], home[...][:, 0:CAPACITY], NT)
        value = pair[:, 0:1] + pair[:, 8:9]
        for k in range(2):
            gate_total[k] = gate_total[k] + jnp.where(routes[k] == float(ORDER[o]), value, 0.0)
    out_ref[...] = total.astype(jnp.bfloat16)
    for k in range(2):
        ggrad_ref[k:k + 1, :] = gate_total[k].T[0:1]

    for o in range(GROUP):
        for k in range(2):
            for d in range(1, his):
                to_hi(o, k, d).wait_send()
            for h in range(his):
                to_mate(o, k, h).wait_send()
            if o > 0:
                to_node(o, k).wait_send()
        if o > 0:
            to_home(o).wait_send()
            gate_home(o).wait_send()
    for b in range(BATCHES):
        gate_mate(b).wait_send()
        for h in range(his):
            sum_mate(b, h).wait_send()
        for d in range(1, his):
            sum_hi(b, d).wait_send()
            gate_hi(b, d).wait_send()


def body(nodes, locals_, layer_input, output_grad, gate_weight, up_weight, down_weight, route, fixed):
    tokens, feat = layer_input.shape
    width, hidden = gate_weight.shape[1:]
    his = locals_ // 2
    bf16, f32, i32 = jnp.bfloat16, jnp.float32, jnp.int32
    vmem, dma = pltpu.VMEM, pltpu.SemaphoreType.DMA
    routed, rows = GROUP * CAPACITY, PAIR * CAPACITY
    scratch = [
        vmem((tokens, feat), bf16),
        vmem((tokens, feat), bf16),
        vmem((width, 2 * hidden), bf16),
        vmem((hidden, width), bf16),
        vmem((2, tokens), i32),
        vmem((2, tokens), i32),
        vmem((GROUP, tokens, CAPACITY), bf16),
        vmem((GROUP, 2, CAPACITY, feat), bf16),
        vmem((BATCHES, locals_, 2, rows, feat), bf16),
        vmem((BATCHES, his, rows, feat), bf16),
        vmem((BATCHES, his, rows, feat), bf16),
        vmem((BATCHES, his, rows, feat), bf16),
        vmem((BATCHES, his, rows, feat), bf16),
        vmem((BATCHES, rows, feat), f32),
        vmem((BATCHES, rows, feat), bf16),
        vmem((BATCHES, rows, feat), bf16),
        vmem((BATCHES, PAIR * 16, LANES), bf16),
        vmem((BATCHES, PAIR * 16, LANES), bf16),
        vmem((BATCHES, PAIR * 16, LANES), bf16),
        vmem((BATCHES, his, PAIR * 16, LANES), bf16),
        vmem((BATCHES, PAIR * 16, LANES), bf16),
        vmem((BATCHES, PAIR * 16, LANES), bf16),
        dma((7,)),
        dma((GROUP, 2)),
        dma((GROUP, 2)),
        dma((GROUP, 2, his)),
        dma((GROUP, 2, his)),
        dma((GROUP, 2, his)),
        dma((GROUP, 2, his)),
        dma((GROUP, his)),
        dma((GROUP, his)),
        dma((GROUP, his)),
        dma((GROUP, his)),
        dma((GROUP,)),
        dma((GROUP,)),
        dma((GROUP,)),
        dma((GROUP,)),
        dma((GROUP, his)),
        dma((GROUP, his)),
        dma((GROUP,)),
        dma((GROUP,)),
    ]
    in_vmem, anywhere = pl.BlockSpec(memory_space=pltpu.VMEM), pl.BlockSpec(memory_space=pl.ANY)
    grads, gate_grads = pl.pallas_call(
        functools.partial(kernel, nodes, locals_),
        out_shape=(
            jax.ShapeDtypeStruct((tokens, feat), bf16),
            jax.ShapeDtypeStruct((2, tokens), f32),
        ),
        in_specs=[anywhere] * 7,
        out_specs=(in_vmem, in_vmem),
        scratch_shapes=scratch,
        compiler_params=pltpu.CompilerParams(
            collective_id=0, has_side_effects=True, vmem_limit_bytes=60 * 1024 * 1024
        ),
        cost_estimate=pl.CostEstimate(
            flops=10 * routed * width * hidden,
            bytes_accessed=6 * width * hidden + 6 * tokens * feat,
            transcendentals=routed * hidden,
        ),
    )(layer_input, output_grad, gate_weight, up_weight, down_weight, route.T, fixed.T)
    return grads, gate_grads.T


def solution(mesh):
    in_specs = (
        P("node", "local"),
        P("node", "local"),
        P("node", None, "local"),
        P("node", None, "local"),
        P("node", "local", None),
        P("node", None),
        P("node", None),
    )
    out_specs = (P("node", "local"), P("node", None))
    run = functools.partial(body, mesh.shape["node"], mesh.shape["local"])
    return jax.shard_map(run, mesh=mesh, in_specs=in_specs, out_specs=out_specs, check_vma=False)
```

time: 65.2 us -> 84.8 us (1.30)
  the two profiles are of different devices: /device:TPU:3 before, /device:TPU:26 now
where the time goes in v5:
time: 84.8 us; the launch traced here: 84 us
  Pallas kernels  80.5 us (95%)
  local copies, waits for them, and re-layouts  2.84 us (3%)
    pallas_call x1, Pallas kernels, body(): pl.pallas_call(functools.partial(kernel, nodes, locals_), out_shape=(jax....  80.5 us
    unnamed x2, local copies, waits for them, and re-layouts  2.84 us

profile of v5, /device:TPU:26, one launch (start us, length us, event | category | flops | bytes accessed | tf_op | source)
XLA Modules:
  0.0 84.0 jit_solution(17288870613374980778)
XLA Ops:
  0.6 80.5 %shard_map.86 = (bf16[128,896]{1,0:T(8,128)(2,1)}, f32[2,128]{1,0:T(2,128)}) custom-call(bf16[128,896]{1,0:T(8,128)(2,1)} %x_hbm.1, bf16[128,896]{1,0:T(8,128)(2,1)} %g_hbm.1, bf16[1,3584,256]{2,1,0:T(8,128)(2,1)} %gate_hbm.1, bf16[1,3584,256]{2,1,0:T(8,128)(2,1)} %up_hbm.1, bf16[1,256,3584]{2,1,0:T(8,128)(2,1)} %down_hbm.1, s32[2,128]{1,0:T(2,128)} %bitcast.4, ...), custom_call_target="tpu_custom_call" | custom-call | flops 2936012800 | bytes 6193152 | tf_op jit(solution)/shard_map/pallas_call | solution.py:423
  81.2 1.6 %copy.11 = bf16[128,896]{1,0:T(8,128)(2,1)} copy(bf16[128,896]{1,0:T(8,128)(2,1)} %get-tuple-element.8) | data formatting | bytes 458752
  82.8 1.2 %copy.12 = f32[128,2]{0,1:T(2,128)} copy(f32[128,2]{0,1:T(2,128)} %bitcast.3) | data formatting | bytes 2048

commit v6 on v2

--- a/solution.py
+++ b/solution.py
@@ -45,12 +45,13 @@
     nodes, locals_,
     x_hbm, g_hbm, gate_hbm, up_hbm, down_hbm, route_hbm, fixed_hbm,
     out_ref, ggrad_ref,
-    x_ref, g_ref, gw, uw, dw, route_ref, fixed_ref,
+    x_ref, g_ref, gu, dw, route_ref, fixed_ref,
     table, packed, got, out_a, in_a, out_b, in_b, mine, out_h, in_h,
     gate_out_a, gate_in_a, gate_out_b, gate_in_b, gate_out_h, gate_in_h,
     wsem, ns, nr, hs, hr, ls, lr, sa, ra, sb, rb, sm, rm, sga, rga, sgb, rgb, sgm, rgm,
 ):
     tokens, feat = x_ref.shape
+    hidden = dw.shape[0]
     his = locals_ // 2
     node, me = lax.axis_index("node"), lax.axis_index("local")
     hi, lo = me // 2, me % 2
@@ -69,10 +70,12 @@
         pltpu.make_async_copy(source, dest, wsem.at[i])
         for i, (source, dest) in enumerate((
             (route_hbm, route_ref), (x_hbm, x_ref), (g_hbm, g_ref), (fixed_hbm, fixed_ref),
-            (gate_hbm.at[0], gw), (up_hbm.at[0], uw), (down_hbm.at[0], dw),
+            (gate_hbm.at[0], gu.at[:, pl.ds(0, hidden)]),
+            (up_hbm.at[0], gu.at[:, pl.ds(hidden, hidden)]),
+            (down_hbm.at[0], dw),
         ))
     ]
-    for copy in fetches:
+    for copy in fetches[:4]:
         copy.start()
 
     barrier = pltpu.get_barrier_semaphore()
@@ -178,6 +181,8 @@
         for k in range(2):
             packed[o, k] = pack(o, k)
             to_node(o, k).start()
+    for copy in fetches[4:]:
+        copy.start()
     for k in range(2):
         to_mate(0, k, hi).start()
     for copy in fetches[3:]:
@@ -193,50 +198,42 @@
     def block(l):
         return pl.ds(pl.multiple_of(l * feat, 64), feat)
 
-    def arrivals(o, k, add):
-        add(me)
-        from_mate(o, k, hi).wait_recv()
-        add(mate)
-        for d in range(1, his):
-            h = turned(d)
+    def pass_on(o, k):
+        for d in range(1, his):
             from_hi(o, k, d).wait_recv()
-            to_mate(o, k, h).start()
-            add(h * 2 + lo)
+            to_mate(o, k, turned(d)).start()
+
+    def gathered(o, k):
+        for h in range(his):
             from_mate(o, k, h).wait_recv()
-            add(h * 2 + 1 - lo)
 
     def compute(o):
-        sums = [jnp.zeros((CAPACITY, gw.shape[1]), jnp.float32) for _ in range(3)]
-
-        def add_input(l):
-            x = got[o, l, 0]
-            sums[0] = sums[0] + dot(x, gw[block(l), :])
-            sums[1] = sums[1] + dot(x, uw[block(l), :])
-
-        def add_grad(l):
-            if feat % LANES == 0:
-                rows = pl.ds(pl.multiple_of(l * feat, LANES), feat)
-                sums[2] = sums[2] + dot(got[o, l, 1], dw[:, rows], NT)
-
-        arrivals(o, 0, add_input)
-        arrivals(o, 1, add_grad)
-        if feat % LANES:
-            for l in range(locals_):
-                sums[2] = sums[2] + dot(got[o, l, 1], dw[:, pl.ds(l * feat, feat)], NT)
-        a, b, v = sums
+        pass_on(o, 0)
+
+        @pl.when(o >= 1)
+        def _():
+            add_hi(o - 1)
+
+        gathered(o, 0)
+        both = jnp.zeros((CAPACITY, 2 * hidden), jnp.float32)
+        for l in range(locals_):
+            both = both + dot(got[o, l, 0], gu[pl.ds(l * feat, feat), :])
+        pass_on(o, 1)
+        gathered(o, 1)
+        v = jnp.zeros((CAPACITY, hidden), jnp.float32)
+        for l in range(locals_):
+            v = v + dot(got[o, l, 1], dw[:, pl.ds(l * feat, feat)], NT)
+        a, b = both[:, 0:hidden], both[:, hidden:2 * hidden]
         s = 1.0 / (1.0 + jnp.exp(-a))
         swish = a * s
         u = (v * swish).astype(jnp.bfloat16)
         w = (v * b * s * (1.0 + a * (1.0 - s))).astype(jnp.bfloat16)
+        grads = jnp.concatenate((w, u), axis=1)
         gate_out_a[o] = split_gate(lay_down(jnp.sum(swish * b * v, axis=1, keepdims=True)))
         gate_mate(o).start()
 
-        @pl.when(o >= 1)
-        def _():
-            add_hi(o - 1)
-
         def back(l):
-            return dot(w, gw[block(l), :], NT) + dot(u, uw[block(l), :], NT)
+            return dot(grads, gu[block(l), :], NT)
 
         def send_mate(h):
             out_a[o, h] = back(h * 2 + 1 - lo).astype(jnp.bfloat16)
@@ -352,8 +349,7 @@
     scratch = [
         vmem((tokens, feat), bf16),
         vmem((tokens, feat), bf16),
-        vmem((width, hidden), bf16),
-        vmem((width, hidden), bf16),
+        vmem((width, 2 * hidden), bf16),
         vmem((hidden, width), bf16),
         vmem((2, tokens), i32),
         vmem((2, tokens), i32),

time: 65.2 us -> 70.6 us (1.083)
  Pallas kernels: 61.5 us -> 66.9 us
    pallas_call x1, Pallas kernels: 61.5 us -> 66.9 us  [body(): pl.pallas_call(functools.partial(kernel, nodes, locals_), out_shape=(jax....]
where the time goes in v6:
time: 70.6 us; the launch traced here: 70.4 us
  Pallas kernels  66.9 us (95%)
  local copies, waits for them, and re-layouts  2.84 us (4%)
    pallas_call x1, Pallas kernels, body(): pl.pallas_call(functools.partial(kernel, nodes, locals_), out_shape=(jax....  66.9 us
    unnamed x2, local copies, waits for them, and re-layouts  2.84 us

profile of v6, /device:TPU:3, one launch (start us, length us, event | category | flops | bytes accessed | tf_op | source)
XLA Modules:
  0.0 70.4 jit_solution(336832401623405685)
XLA Ops:
  0.6 66.9 %shard_map.86 = (bf16[128,896]{1,0:T(8,128)(2,1)}, f32[2,128]{1,0:T(2,128)}) custom-call(bf16[128,896]{1,0:T(8,128)(2,1)} %x_hbm.1, bf16[128,896]{1,0:T(8,128)(2,1)} %g_hbm.1, bf16[1,3584,256]{2,1,0:T(8,128)(2,1)} %gate_hbm.1, bf16[1,3584,256]{2,1,0:T(8,128)(2,1)} %up_hbm.1, bf16[1,256,3584]{2,1,0:T(8,128)(2,1)} %down_hbm.1, s32[2,128]{1,0:T(2,128)} %bitcast.4, ...), custom_call_target="tpu_custom_call" | custom-call | flops 2936012800 | bytes 6193152 | tf_op jit(solution)/shard_map/pallas_call | solution.py:393
  67.5 1.6 %copy.11 = bf16[128,896]{1,0:T(8,128)(2,1)} copy(bf16[128,896]{1,0:T(8,128)(2,1)} %get-tuple-element.8) | data formatting | bytes 458752
  69.2 1.2 %copy.12 = f32[128,2]{0,1:T(2,128)} copy(f32[128,2]{0,1:T(2,128)} %bitcast.3) | data formatting | bytes 2048

commit v7 on v1

--- a/solution.py
+++ b/solution.py
@@ -37,11 +37,15 @@
     return jnp.sum(jnp.where(keep, parts.astype(jnp.float32), 0.0), axis=1, keepdims=True)
 
 
+def stand_up(row):
+    return jnp.broadcast_to(row, (LANES, row.shape[1])).T
+
+
 def kernel(
     nodes, locals_,
-    x_ref, g_ref, gate_hbm, up_hbm, down_hbm, route_ref, fixed_ref,
+    x_hbm, g_hbm, gate_hbm, up_hbm, down_hbm, route_hbm, fixed_hbm,
     out_ref, ggrad_ref,
-    gw, uw, dw, table, packed, got, out_a, in_a, own, own_gate, out_b, in_b, mine, out_h, in_h,
+    x_ref, g_ref, route_ref, fixed_ref, gw, uw, dw, table, packed, got, out_a, in_a, own, own_gate, out_b, in_b, mine, out_h, in_h,
     wsem, ns, nr, hs, hr, ls, lr, sa, ra, sb, rb, sm, rm,
 ):
     tokens, feat = x_ref.shape
@@ -61,11 +65,14 @@
     def turned(d):
         return lax.rem(hi + d, his)
 
-    weights = [
-        pltpu.make_async_copy(source.at[0], dest, wsem.at[i])
-        for i, (source, dest) in enumerate(((gate_hbm, gw), (up_hbm, uw), (down_hbm, dw)))
+    fetches = [
+        pltpu.make_async_copy(source, dest, wsem.at[i])
+        for i, (source, dest) in enumerate((
+            (route_hbm, route_ref), (x_hbm, x_ref), (g_hbm, g_ref), (fixed_hbm, fixed_ref),
+            (gate_hbm.at[0], gw), (up_hbm.at[0], uw), (down_hbm.at[0], dw),
+        ))
     ]
-    for copy in weights:
+    for copy in fetches:
         copy.start()
 
     barrier = pltpu.get_barrier_semaphore()
@@ -117,9 +124,10 @@
     def to_home(o):
         return remote(out_h.at[o], in_h.at[o], sm.at[o], rm.at[o], ahead(-o))
 
-    route = route_ref[...]
-    lanes = lane_index(tokens)
-    chosen = ((route[:, 0:1] == lanes) | (route[:, 1:2] == lanes)).astype(jnp.float32)
+    fetches[0].wait()
+    lanes = lane_index(tokens).astype(jnp.float32)
+    routes = [stand_up(route_ref[k:k + 1, :].astype(jnp.float32)) for k in range(2)]
+    chosen = ((routes[0] == lanes) | (routes[1] == lanes)).astype(jnp.float32)
     row = lax.broadcasted_iota(jnp.int32, (tokens, tokens), 0)
     column = lax.broadcasted_iota(jnp.int32, (tokens, tokens), 1)
     below = (column <= row).astype(jnp.float32).astype(jnp.bfloat16)
@@ -136,6 +144,7 @@
         return dot(tables[o], source[...], TN).astype(jnp.bfloat16)
 
     for k in range(2):
+        fetches[1 + k].wait()
         got[0, me, k] = pack(0, k)
     pl.semaphore_wait(barrier, len(friends))
     for k in range(2):
@@ -147,7 +156,7 @@
             to_node(o, k).start()
     for k in range(2):
         to_mate(0, k, hi).start()
-    for copy in weights:
+    for copy in fetches[3:]:
         copy.wait()
 
     def spread(o):
@@ -219,6 +228,10 @@
             to_home(o).start()
 
     def step(i, carry):
+        @pl.when(i >= 1)
+        def _():
+            add_mate(i - 1)
+
         @pl.when(i + 1 < GROUP)
         def _():
             spread(i + 1)
@@ -227,13 +240,9 @@
         def _():
             pass_on(i)
 
-        @pl.when((i >= 1) & (i <= GROUP))
-        def _():
-            add_mate(i - 1)
-
-        @pl.when(i >= 2)
-        def _():
-            add_hi(i - 2)
+        @pl.when(i >= 1)
+        def _():
+            add_hi(i - 1)
 
         @pl.when(i < GROUP)
         def _():
@@ -241,22 +250,24 @@
 
         return carry
 
-    lax.fori_loop(0, GROUP + 2, step, 0)
-
-    gates = fixed_ref[...].astype(jnp.float32) / 65536.0
+    lax.fori_loop(0, GROUP + 1, step, 0)
+
+    gates = [stand_up(fixed_ref[k:k + 1, :].astype(jnp.float32)) / 65536.0 for k in range(2)]
     total = jnp.zeros((tokens, feat), jnp.float32)
-    gate_total = jnp.zeros(gates.shape, jnp.float32)
+    gate_total = [jnp.zeros((tokens, LANES), jnp.float32) for _ in range(2)]
     for o in range(GROUP):
         if o > 0:
             to_home(o).wait_recv()
         home = out_h if o == 0 else in_h
-        hits = route == o
-        weight = jnp.sum(jnp.where(hits, gates, 0.0), axis=1, keepdims=True)
+        hits = [routes[k] == float(o) for k in range(2)]
+        weight = sum(jnp.where(hits[k], gates[k], 0.0) for k in range(2))[:, 0:1]
         total = total + weight * dot(table[o], home[o, :, pl.ds(0, feat)])
         back_gate = join_gate(dot(table[o], home[o, :, gate_lanes]))
-        gate_total = gate_total + jnp.where(hits, back_gate, 0.0)
+        for k in range(2):
+            gate_total[k] = gate_total[k] + jnp.where(hits[k], back_gate, 0.0)
     out_ref[...] = total.astype(jnp.bfloat16)
-    ggrad_ref[...] = gate_total
+    for k in range(2):
+        ggrad_ref[k:k + 1, :] = gate_total[k].T[0:1]
 
     def finish(o, carry):
         for k in range(2):
@@ -287,6 +298,10 @@
     bf16, f32 = jnp.bfloat16, jnp.float32
     vmem, dma = pltpu.VMEM, pltpu.SemaphoreType.DMA
     scratch = [
+        vmem((tokens, feat), bf16),
+        vmem((tokens, feat), bf16),
+        vmem((2, tokens), jnp.int32),
+        vmem((2, tokens), jnp.int32),
         vmem((width, hidden), bf16),
         vmem((width, hidden), bf16),
         vmem((hidden, width), bf16),
@@ -302,7 +317,7 @@
         vmem((GROUP, CAPACITY, feat), f32),
         vmem((GROUP, CAPACITY, wide), bf16),
         vmem((GROUP, CAPACITY, wide), bf16),
-        dma((3,)),
+        dma((7,)),
         dma((GROUP, 2)),
         dma((GROUP, 2)),
         dma((GROUP, 2, his)),
@@ -318,24 +333,25 @@
     ]
     in_vmem, anywhere = pl.BlockSpec(memory_space=pltpu.VMEM), pl.BlockSpec(memory_space=pl.ANY)
     routed = GROUP * CAPACITY
-    return pl.pallas_call(
+    grads, gate_grads = pl.pallas_call(
         functools.partial(kernel, nodes, locals_),
         out_shape=(
             jax.ShapeDtypeStruct((tokens, feat), bf16),
-            jax.ShapeDtypeStruct(fixed.shape, f32),
+            jax.ShapeDtypeStruct((2, tokens), f32),
         ),
-        in_specs=[in_vmem, in_vmem, anywhere, anywhere, anywhere, in_vmem, in_vmem],
+        in_specs=[anywhere] * 7,
         out_specs=(in_vmem, in_vmem),
         scratch_shapes=scratch,
         compiler_params=pltpu.CompilerParams(
-            collective_id=0, has_side_effects=True, vmem_limit_bytes=48 * 1024 * 1024
+            collective_id=0, has_side_effects=True, vmem_limit_bytes=60 * 1024 * 1024
         ),
         cost_estimate=pl.CostEstimate(
             flops=10 * routed * width * hidden,
             bytes_accessed=6 * width * hidden + 6 * tokens * feat,
             transcendentals=routed * hidden,
         ),
-    )(layer_input, output_grad, gate_weight, up_weight, down_weight, route, fixed)
+    )(layer_input, output_grad, gate_weight, up_weight, down_weight, route.T, fixed.T)
+    return grads, gate_grads.T
 
 
 def solution(mesh):

time: 66.8 us -> 69.9 us (1.046)
  the two profiles are of different devices: /device:TPU:26 before, /device:TPU:3 now
where the time goes in v7:
time: 69.9 us; the launch traced here: 69.7 us
  Pallas kernels  66.3 us (95%)
  local copies, waits for them, and re-layouts  2.84 us (4%)
    pallas_call x1, Pallas kernels, body(): pl.pallas_call(functools.partial(kernel, nodes, locals_), out_shape=(jax....  66.3 us
    unnamed x2, local copies, waits for them, and re-layouts  2.84 us

profile of v7, /device:TPU:3, one launch (start us, length us, event | category | flops | bytes accessed | tf_op | source)
XLA Modules:
  0.0 69.7 jit_solution(16056563144048643981)
XLA Ops:
  0.6 66.3 %shard_map.86 = (bf16[128,896]{1,0:T(8,128)(2,1)}, f32[2,128]{1,0:T(2,128)}) custom-call(bf16[128,896]{1,0:T(8,128)(2,1)} %x_hbm.1, bf16[128,896]{1,0:T(8,128)(2,1)} %g_hbm.1, bf16[1,3584,256]{2,1,0:T(8,128)(2,1)} %gate_hbm.1, bf16[1,3584,256]{2,1,0:T(8,128)(2,1)} %up_hbm.1, bf16[1,256,3584]{2,1,0:T(8,128)(2,1)} %down_hbm.1, s32[2,128]{1,0:T(2,128)} %bitcast.4, ...), custom_call_target="tpu_custom_call" | custom-call | flops 2936012800 | bytes 6193152 | tf_op jit(solution)/shard_map/pallas_call | solution.py:336
  66.9 1.6 %copy.11 = bf16[128,896]{1,0:T(8,128)(2,1)} copy(bf16[128,896]{1,0:T(8,128)(2,1)} %get-tuple-element.8) | data formatting | bytes 458752
  68.5 1.2 %copy.12 = f32[128,2]{0,1:T(2,128)} copy(f32[128,2]{0,1:T(2,128)} %bitcast.3) | data formatting | bytes 2048

commit v8 on v7

--- a/solution.py
+++ b/solution.py
@@ -228,29 +228,29 @@
             to_home(o).start()
 
     def step(i, carry):
-        @pl.when(i >= 1)
+        @pl.when(i + 1 < GROUP)
+        def _():
+            spread(i + 1)
+
+        @pl.when(i < GROUP)
+        def _():
+            pass_on(i)
+
+        @pl.when((i >= 1) & (i <= GROUP))
         def _():
             add_mate(i - 1)
 
-        @pl.when(i + 1 < GROUP)
-        def _():
-            spread(i + 1)
+        @pl.when(i >= 2)
+        def _():
+            add_hi(i - 2)
 
         @pl.when(i < GROUP)
         def _():
-            pass_on(i)
-
-        @pl.when(i >= 1)
-        def _():
-            add_hi(i - 1)
-
-        @pl.when(i < GROUP)
-        def _():
             compute(i)
 
         return carry
 
-    lax.fori_loop(0, GROUP + 1, step, 0)
+    lax.fori_loop(0, GROUP + 2, step, 0)
 
     gates = [stand_up(fixed_ref[k:k + 1, :].astype(jnp.float32)) / 65536.0 for k in range(2)]
     total = jnp.zeros((tokens, feat), jnp.float32)

time: 69.9 us -> 62.7 us (0.90)
  the two profiles are of different devices: /device:TPU:3 before, /device:TPU:26 now
where the time goes in v8:
time: 62.7 us; the launch traced here: 62.5 us
  Pallas kernels  59 us (94%)
  local copies, waits for them, and re-layouts  2.84 us (5%)
  between operations  0.64 us (1%)
    pallas_call x1, Pallas kernels, body(): pl.pallas_call(functools.partial(kernel, nodes, locals_), out_shape=(jax....  59 us
    unnamed x2, local copies, waits for them, and re-layouts  2.84 us

profile of v8, /device:TPU:26, one launch (start us, length us, event | category | flops | bytes accessed | tf_op | source)
XLA Modules:
  0.0 62.5 jit_solution(14879619132964323876)
XLA Ops:
  0.6 59.0 %shard_map.86 = (bf16[128,896]{1,0:T(8,128)(2,1)}, f32[2,128]{1,0:T(2,128)}) custom-call(bf16[128,896]{1,0:T(8,128)(2,1)} %x_hbm.1, bf16[128,896]{1,0:T(8,128)(2,1)} %g_hbm.1, bf16[1,3584,256]{2,1,0:T(8,128)(2,1)} %gate_hbm.1, bf16[1,3584,256]{2,1,0:T(8,128)(2,1)} %up_hbm.1, bf16[1,256,3584]{2,1,0:T(8,128)(2,1)} %down_hbm.1, s32[2,128]{1,0:T(2,128)} %bitcast.4, ...), custom_call_target="tpu_custom_call" | custom-call | flops 2936012800 | bytes 6193152 | tf_op jit(solution)/shard_map/pallas_call | solution.py:336
  59.7 1.6 %copy.11 = bf16[128,896]{1,0:T(8,128)(2,1)} copy(bf16[128,896]{1,0:T(8,128)(2,1)} %get-tuple-element.8) | data formatting | bytes 458752
  61.3 1.2 %copy.12 = f32[128,2]{0,1:T(2,128)} copy(f32[128,2]{0,1:T(2,128)} %bitcast.3) | data formatting | bytes 2048

commit v9 on v8

--- a/solution.py
+++ b/solution.py
@@ -228,6 +228,10 @@
             to_home(o).start()
 
     def step(i, carry):
+        @pl.when((i >= 1) & (i <= GROUP))
+        def _():
+            add_mate(i - 1)
+
         @pl.when(i + 1 < GROUP)
         def _():
             spread(i + 1)
@@ -235,10 +239,6 @@
         @pl.when(i < GROUP)
         def _():
             pass_on(i)
-
-        @pl.when((i >= 1) & (i <= GROUP))
-        def _():
-            add_mate(i - 1)
 
         @pl.when(i >= 2)
         def _():

time: 62.7 us -> 65.2 us (1.040)
  Pallas kernels: 59 us -> 60.9 us
    pallas_call x1, Pallas kernels: 59 us -> 60.9 us  [body(): pl.pallas_call(functools.partial(kernel, nodes, locals_), out_shape=(jax....]
where the time goes in v9:
time: 65.2 us; the launch traced here: 64.4 us
  Pallas kernels  60.9 us (93%)
  local copies, waits for them, and re-layouts  2.84 us (4%)
    pallas_call x1, Pallas kernels, body(): pl.pallas_call(functools.partial(kernel, nodes, locals_), out_shape=(jax....  60.9 us
    unnamed x2, local copies, waits for them, and re-layouts  2.84 us

profile of v9, /device:TPU:26, one launch (start us, length us, event | category | flops | bytes accessed | tf_op | source)
XLA Modules:
  0.0 64.4 jit_solution(12171045334103465077)
XLA Ops:
  0.6 60.9 %shard_map.86 = (bf16[128,896]{1,0:T(8,128)(2,1)}, f32[2,128]{1,0:T(2,128)}) custom-call(bf16[128,896]{1,0:T(8,128)(2,1)} %x_hbm.1, bf16[128,896]{1,0:T(8,128)(2,1)} %g_hbm.1, bf16[1,3584,256]{2,1,0:T(8,128)(2,1)} %gate_hbm.1, bf16[1,3584,256]{2,1,0:T(8,128)(2,1)} %up_hbm.1, bf16[1,256,3584]{2,1,0:T(8,128)(2,1)} %down_hbm.1, s32[2,128]{1,0:T(2,128)} %bitcast.4, ...), custom_call_target="tpu_custom_call" | custom-call | flops 2936012800 | bytes 6193152 | tf_op jit(solution)/shard_map/pallas_call | solution.py:336
  61.6 1.6 %copy.11 = bf16[128,896]{1,0:T(8,128)(2,1)} copy(bf16[128,896]{1,0:T(8,128)(2,1)} %get-tuple-element.8) | data formatting | bytes 458752
  63.2 1.2 %copy.12 = f32[128,2]{0,1:T(2,128)} copy(f32[128,2]{0,1:T(2,128)} %bitcast.3) | data formatting | bytes 2048
